TPU v7x, 128 devices: a whole 4x4x4 slice. The times are simulated.
128 devices in a mesh: gx: 8 (over z_hi, x), gy: 16 (over y, z_lo, core).
Axes of the slice: x: 4, y: 4, z: 4 (z_hi: 2, z_lo: 2; z = z_hi * 2 + z_lo), core: 2. Of those that a mesh axis runs over, the one named last changes fastest.
Arguments:
- latent: bfloat16 [256, 1024, 512], P('gx', 'gy'), may hold values from -6 to 6
- cotangent: bfloat16 [256, 1024, 512], P('gx', 'gy'), may hold values from -6 to 6
- layer_norm_gain: float32 [512], replicated, may hold values from 0.1 to 1.9
- layer_norm_bias: float32 [512], replicated, may hold values from -3 to 3
- w_qkv: bfloat16 [512, 1536], replicated, may hold values from -0.25 to 0.25
- w_out: bfloat16 [512, 512], replicated, may hold values from -0.25 to 0.25
- rel_bias: float32 [16, 225], replicated, may hold values from -2 to 250
Outputs:
- latent_gradient: bfloat16 [256, 1024, 512], P('gx', 'gy')
- d_w_qkv: float32 [512, 1536], replicated
- d_w_out: float32 [512, 512], replicated
- d_ln_gain: float32 [512], replicated
- d_ln_bias: float32 [512], replicated
All inputs are finite; a program needn't handle non-finite values.
Results may differ from a plain program's by a relative error of at most 0.0097.
Values may be sent and summed in bfloat16 or wider, within the bound.
No kernel may reach another device: no remote copies, remote signals or barrier semaphores. Data moves between devices by JAX's collectives and lax.ppermute only.
A program may use at most 192 MiB of HBM per device.

v0:
```python
import math

import jax
import jax.numpy as jnp
from jax import lax
from jax.sharding import PartitionSpec as P


def bias_table(rel_bias):
    position = jnp.arange(64, dtype=jnp.int32)
    prow = position // 8
    pcol = position % 8
    offset = (prow[:, None] - prow[None, :] + 7) * 15 + (pcol[:, None] - pcol[None, :] + 7)
    onehot = (offset.reshape(1, 4096) == jnp.arange(225, dtype=jnp.int32)[:, None]).astype(
        jnp.float32
    )
    full = jnp.dot(rel_bias, onehot, precision=lax.Precision.HIGHEST)
    return full.reshape(rel_bias.shape[0], 64, 64)


def contract_rows(left, right):
    return lax.dot_general(
        left, right, (((0,), (0,)), ((), ())), preferred_element_type=jnp.float32
    )


def contract_cols(left, right):
    return lax.dot_general(
        left, right, (((1,), (1,)), ((), ())), preferred_element_type=jnp.float32
    )


def window_backward(
    latent_w, weight_cotangent, layer_norm_gain, layer_norm_bias, w_qkv, w_out, bias_full
):
    count, width = (latent_w.shape[0], latent_w.shape[2])
    heads = bias_full.shape[0]
    head_dim = width // heads
    factor = 1.0 / math.sqrt(head_dim)
    values = latent_w.astype(jnp.float32)
    centre = jnp.mean(values, -1, keepdims=True)
    centred_latent = values - centre
    variance = jnp.mean(centred_latent * centred_latent, -1, keepdims=True)
    inverse_deviation = lax.rsqrt(variance + 1e-05)
    standardised_latent = centred_latent * inverse_deviation
    normed_latent = (standardised_latent * layer_norm_gain + layer_norm_bias).astype(jnp.bfloat16)
    flat_normed = normed_latent.reshape(-1, width)
    qkv = jnp.dot(flat_normed, w_qkv, preferred_element_type=jnp.float32).astype(jnp.bfloat16)
    qkv = qkv.reshape(count, 64, 3, heads, head_dim)
    query = qkv[:, :, 0]
    keys = qkv[:, :, 1]
    vals = qkv[:, :, 2]
    scores = (
        jnp.einsum("wqhd,wkhd->whqk", query, keys, preferred_element_type=jnp.float32) * factor
        + bias_full[None]
    )
    highest = jnp.max(scores, -1, keepdims=True)
    probs = jnp.exp(scores - highest)
    probs = probs / jnp.sum(probs, -1, keepdims=True)
    probs_b = probs.astype(jnp.bfloat16)
    attended = (
        jnp.einsum("whqk,wkhd->wqhd", probs_b, vals, preferred_element_type=jnp.float32)
        .astype(jnp.bfloat16)
        .reshape(-1, width)
    )
    cot_flat = weight_cotangent.reshape(-1, width)
    grad_out = contract_rows(attended, cot_flat)
    d_att = contract_cols(cot_flat, w_out).astype(jnp.bfloat16).reshape(count, 64, heads, head_dim)
    d_probs = jnp.einsum("wqhd,wkhd->whqk", d_att, vals, preferred_element_type=jnp.float32)
    d_vals = jnp.einsum("whqk,wqhd->wkhd", probs_b, d_att, preferred_element_type=jnp.float32)
    d_scores = probs * (d_probs - jnp.sum(probs * d_probs, -1, keepdims=True))
    ds_b = d_scores.astype(jnp.bfloat16)
    d_query = jnp.einsum("whqk,wkhd->wqhd", ds_b, keys, preferred_element_type=jnp.float32) * factor
    d_keys = jnp.einsum("whqk,wqhd->wkhd", ds_b, query, preferred_element_type=jnp.float32) * factor
    d_qkv = jnp.stack([d_query, d_keys, d_vals], axis=2).astype(jnp.bfloat16).reshape(-1, 3 * width)
    grad_qkv = contract_rows(flat_normed, d_qkv)
    normed_gradient = contract_cols(d_qkv, w_qkv).reshape(count, 64, width)
    gain_gradient = jnp.sum(standardised_latent * normed_gradient, axis=(0, 1))
    grad_bias = jnp.sum(normed_gradient, axis=(0, 1))
    normalised_gradient = normed_gradient * layer_norm_gain
    latent_gradient = weight_cotangent.astype(jnp.float32) + inverse_deviation * (
        normalised_gradient
        - jnp.mean(normalised_gradient, -1, keepdims=True)
        - standardised_latent
        * jnp.mean(normalised_gradient * standardised_latent, -1, keepdims=True)
    )
    return (latent_gradient.astype(jnp.bfloat16), grad_qkv, grad_out, gain_gradient, grad_bias)


def body(latent, cotangent, layer_norm_gain, layer_norm_bias, w_qkv, w_out, rel_bias):
    rows, cols, width = latent.shape
    count_x = lax.axis_size("gx")
    count_y = lax.axis_size("gy")
    upper_x = max(count_x, 8) // count_x
    lower_x = rows // (upper_x * count_x)
    group_x = max(count_x, 8) // 8
    upper_y = max(count_y, 8) // count_y
    lower_y = cols // (upper_y * count_y)
    group_y = max(count_y, 8) // 8
    stacked = jnp.stack([latent, cotangent]).reshape(
        2, upper_x, count_x, lower_x, upper_y, count_y, lower_y, width
    )
    moved = lax.all_to_all(
        lax.all_to_all(stacked, "gx", split_axis=2, concat_axis=2, tiled=True),
        "gy",
        split_axis=5,
        concat_axis=5,
        tiled=True,
    )
    arranged = moved.transpose(0, 2, 1, 3, 5, 4, 6, 7)
    arranged = arranged.reshape(2, 8, group_x, lower_x, 8, group_y, lower_y, width)
    arranged = arranged.transpose(0, 2, 3, 5, 6, 1, 4, 7).reshape(2, -1, 64, width)
    bias_full = bias_table(rel_bias)
    d_window, grad_qkv, grad_out, gain_gradient, grad_bias = window_backward(
        arranged[0], arranged[1], layer_norm_gain, layer_norm_bias, w_qkv, w_out, bias_full
    )
    sums = lax.psum((grad_qkv, grad_out, gain_gradient, grad_bias), ("gx", "gy"))
    norm = 1.0 / math.sqrt(rows * cols * count_x * count_y)
    back = d_window.reshape(group_x, lower_x, group_y, lower_y, 8, 8, width).transpose(
        4, 0, 1, 5, 2, 3, 6
    )
    back = back.reshape(count_x, upper_x, lower_x, count_y, upper_y, lower_y, width)
    sending = back.transpose(1, 0, 2, 4, 3, 5, 6)
    returned = lax.all_to_all(
        lax.all_to_all(sending, "gx", split_axis=1, concat_axis=1, tiled=True),
        "gy",
        split_axis=4,
        concat_axis=4,
        tiled=True,
    )
    latent_gradient = returned.reshape(rows, cols, width)
    return (latent_gradient, sums[0] * norm, sums[1] * norm, sums[2] * norm, sums[3] * norm)


def solution(mesh):
    return jax.shard_map(
        body,
        mesh=mesh,
        in_specs=(P("gx", "gy", None), P("gx", "gy", None), P(), P(), P(), P(), P()),
        out_specs=(P("gx", "gy", None), P(), P(), P(), P()),
        check_vma=False,
    )
```

profile of v0, /device:TPU:1, one launch (start us, length us, event | category | flops | bytes accessed | tf_op | source)
XLA Modules:
  0.0 642.0 jit_solution(9786744516092030417)
XLA Ops:
  7.2 4.1 stack.21
  11.3 4.0 stack.22
  15.2 5.4 pad_maximum_fusion
  20.6 3.1 copy.131
  23.7 58.0 %all_to_all.20 = bf16[2,1,8,4,1,16,4,512]{7,6,5,3,4,1,0,2:T(4,128)(2,1)S(1)} all-to-all(bf16[2,1,8,4,1,16,4,512]{7,6,5,3,4,1,0,2:T(4,128)(2,1)S(1)} %copy.131), channel_id=1, replica_groups=mesh['gx'=8,'gy'=16] {'gx'}, dimensions={2} | all-to-all | bytes 8388608 | tf_op jit(solution)/shard_map/all_to_all | solution.py:104
  81.7 4.4 copy.132
  86.0 7.3 %all-to-all-start.1 = ((bf16[2,1,8,4,1,16,4,512]{7,6,3,2,4,1,0,5:T(4,128)(2,1)}), bf16[2,1,8,4,1,16,4,512]{7,6,3,2,4,1,0,5:T(4,128)(2,1)}, u32[]{:S(2)}, u32[]{:S(2)}) async-start(bf16[2,1,8,4,1,16,4,512]{7,6,3,2,4,1,0,5:T(4,128)(2,1)} %copy.132), calls=%async_computation.1 | async-start | bytes 8388608 | tf_op jit(solution)/shard_map/all_to_all | solution.py:103
  95.3 50.6 %all-to-all-done.1 = bf16[2,1,8,4,1,16,4,512]{7,6,3,2,4,1,0,5:T(4,128)(2,1)} async-done(((bf16[2,1,8,4,1,16,4,512]{7,6,3,2,4,1,0,5:T(4,128)(2,1)}), bf16[2,1,8,4,1,16,4,512]{7,6,3,2,4,1,0,5:T(4,128)(2,1)}, u32[]{:S(2)}, u32[]{:S(2)}) %all-to-all-start.1) | async-done | bytes 4194336 | tf_op jit(solution)/shard_map/all_to_all | solution.py:103
  145.9 6.7 %copy.133 = bf16[2,1,8,4,1,16,4,512]{7,2,6,5,3,0,4,1:T(8,128)(2,1)S(1)} copy(bf16[2,1,8,4,1,16,4,512]{7,6,3,2,4,1,0,5:T(4,128)(2,1)} %all-to-all-done.1) | data formatting | bytes 8388608 | tf_op jit(solution)/shard_map/all_to_all | solution.py:103
  156.1 2.5 multiply_reduce_fusion.3
  160.3 5.6 slice_convert_fusion
  165.9 6.2 copy.138
  175.3 2.6 convolution_convert_fusion.1
  177.9 3.9 copy.144
  181.8 7.1 %reshape.221 = bf16[32,64,16,32]{1,0,3,2:T(8,128)(2,1)} reshape(bf16[2048,512]{0,1:T(8,128)(2,1)} %copy.144) | data formatting | bytes 4194304 | tf_op jit(solution)/shard_map/reshape | solution.py:68
  188.9 2.6 fusion.7
  191.6 5.3 convolution_convert_fusion
  196.9 8.6 %copy.139 = bf16[2048,1536]{0,1:T(8,128)(2,1)} copy(bf16[2048,1536]{1,0:T(8,128)(2,1)} %convolution_convert_fusion) | data formatting | bytes 12582912 | tf_op jit(solution)/shard_map/convert_element_type | solution.py:48
  205.4 18.6 %reshape.220 = bf16[32,64,3,16,32]{1,0,4,3,2:T(8,128)(2,1)} reshape(bf16[2048,1536]{0,1:T(8,128)(2,1)} %copy.139) | data formatting | bytes 12582912 | tf_op jit(solution)/shard_map/reshape | solution.py:49
  224.1 8.1 %fusion.29 = (bf16[32,64,1,16,32]{1,0,4,3,2:T(8,128)(2,1)}, bf16[32,64,1,16,32]{1,0,4,3,2:T(8,128)(2,1)}, bf16[32,64,1,16,32]{1,0,4,3,2:T(8,128)(2,1)S(1)}) fusion(bf16[32,64,3,16,32]{1,0,4,3,2:T(8,128)(2,1)} %reshape.220), kind=kLoop, calls=%fused_computation.65 | loop fusion | bytes 12582912 | tf_op jit(solution)/shard_map/slice | solution.py:52
  234.1 15.6 %fusion.13 = f32[32,16,64,64]{2,3,1,0:T(8,128)} fusion(bf16[32,64,1,16,32]{1,0,4,3,2:T(8,128)(2,1)S(1)} %get-tuple-element.15, bf16[32,64,1,16,32]{1,0,4,3,2:T(8,128)(2,1)} %get-tuple-element.14), kind=kOutput, calls=%fused_computation.36 | convolution fusion | flops 134217728 | bytes 12582912 | tf_op jit(solution)/shard_map/wqhd,wkhd->whqk/dot_general | solution.py:54
  249.7 17.8 %fusion.30 = (f32[32,16,64]{2,1,0:T(8,128)S(1)}, f32[32,16,64,64]{2,3,1,0:T(8,128)}) fusion(f32[32,16,64,64]{2,3,1,0:T(8,128)} %fusion.13, f32[16,64,64]{1,2,0:T(8,128)S(1)} %copy.142), kind=kOutput, calls=%fused_computation.66 | output fusion | flops 12582975 | bytes 17170432 | tf_op jit(solution)/shard_map/sub | solution.py:58
  267.5 10.9 %fusion.18 = bf16[32,64,1,16,32]{1,4,3,0,2:T(8,128)(2,1)} fusion(bf16[32,64,16,32]{1,0,3,2:T(8,128)(2,1)} %reshape.221, f32[32,16,64,64]{2,3,1,0:T(8,128)} %get-tuple-element.20, f32[32,16,64]{2,1,0:T(8,128)S(1)} %get-tuple-element.19), kind=kOutput, calls=%fused_computation.42 | convolution fusion | flops 138412032 | bytes 12713984 | tf_op jit(solution)/shard_map/whqk,wqhd->wkhd/dot_general | solution.py:70
  278.4 13.9 %convert_bitcast_fusion = bf16[32,64,16,32]{1,3,2,0:T(8,128)(2,1)} fusion(bf16[32,64,1,16,32]{1,0,4,3,2:T(8,128)(2,1)} %get-tuple-element.13, f32[32,16,64,64]{2,3,1,0:T(8,128)} %get-tuple-element.20, f32[32,16,64]{2,1,0:T(8,128)S(1)} %get-tuple-element.19), kind=kOutput, calls=%fused_computation.24 | convolution fusion | flops 139460608 | bytes 12713984 | tf_op jit(solution)/shard_map/whqk,wkhd->wqhd/dot_general | solution.py:62
  292.3 14.6 %multiply_reduce_fusion = (f32[32,16,64]{2,1,0:T(8,128)S(1)}, f32[32,16,64,64]{2,3,1,0:T(8,128)}) fusion(f32[32,16,64,64]{2,3,1,0:T(8,128)} %get-tuple-element.20, f32[32,16,64]{2,1,0:T(8,128)S(1)} %get-tuple-element.19, bf16[32,64,1,16,32]{1,0,4,3,2:T(8,128)(2,1)} %get-tuple-element.13, bf16[32,64,16,32]{1,0,3,2:T(8,128)(2,1)} %reshape.221), kind=kOutput, calls=%fused_computation.3 | convolution fusion | flops 140476416 | bytes 21233664 | tf_op jit(solution)/shard_map/wqhd,wkhd->whqk/dot_general | solution.py:69
  306.9 15.3 %multiply_convert_fusion = bf16[32,16,64,64]{2,3,1,0:T(8,128)(2,1)} fusion(f32[32,16,64,64]{2,3,1,0:T(8,128)} %get-tuple-element.22, f32[32,16,64]{2,1,0:T(8,128)S(1)} %get-tuple-element.21, f32[32,16,64,64]{2,3,1,0:T(8,128)} %get-tuple-element.20, f32[32,16,64]{2,1,0:T(8,128)S(1)} %get-tuple-element.19), kind=kLoop, calls=%fused_computation.2 | loop fusion | flops 8388608 | bytes 21233664 | tf_op jit(solution)/shard_map/convert_element_type | solution.py:72
  322.3 11.2 %multiply_bitcast_fusion = bf16[32,64,1,16,32]{1,4,3,0,2:T(8,128)(2,1)} fusion(bf16[32,16,64,64]{2,3,1,0:T(8,128)(2,1)} %multiply_convert_fusion, bf16[32,64,1,16,32]{1,0,4,3,2:T(8,128)(2,1)} %get-tuple-element.14), kind=kOutput, calls=%fused_computation.7 | convolution fusion | flops 136314880 | bytes 8388608 | tf_op jit(solution)/shard_map/whqk,wqhd->wkhd/dot_general | solution.py:74
  333.5 9.7 %multiply_bitcast_fusion.1 = bf16[32,64,1,16,32]{1,4,3,0,2:T(8,128)(2,1)S(1)} fusion(bf16[32,16,64,64]{2,3,1,0:T(8,128)(2,1)} %multiply_convert_fusion, bf16[32,64,1,16,32]{1,0,4,3,2:T(8,128)(2,1)} %copy-done.1), kind=kOutput, calls=%fused_computation.8 | convolution fusion | flops 136314880 | bytes 8388608 | tf_op jit(solution)/shard_map/whqk,wkhd->wqhd/dot_general | solution.py:73
  343.2 3.5 maximum_convert_fusion
  346.7 10.2 %copy.160 = bf16[32,64,3,16,32]{1,0,4,3,2:T(8,128)(2,1)} copy(bf16[32,64,3,16,32]{1,4,3,0,2:T(8,128)(2,1)S(1)} %maximum_convert_fusion) | data formatting | bytes 12582912 | tf_op jit(solution)/shard_map/convert_element_type | solution.py:75
  356.9 5.9 copy.151
  363.8 3.2 copy.159
  367.0 5.8 copy.134
  372.8 4.7 copy.162
  377.4 6.9 %reshape.224 = bf16[2048,512]{0,1:T(8,128)(2,1)} reshape(bf16[32,64,16,32]{1,0,3,2:T(8,128)(2,1)} %copy.162) | data formatting | bytes 4194304 | tf_op jit(solution)/shard_map/reshape | solution.py:64
  384.4 4.4 fusion.32
  388.8 17.9 %convert_element_type.88 = bf16[2048,1536]{0,1:T(8,128)(2,1)} reshape(bf16[32,64,3,16,32]{1,0,4,3,2:T(8,128)(2,1)} %copy.160) | data formatting | bytes 12582912 | tf_op jit(solution)/shard_map/convert_element_type | solution.py:75
  406.8 13.7 %multiply_reduce_fusion.1 = (f32[512]{0:T(512)S(1)}, f32[32,64]{1,0:T(8,128)S(1)}, f32[32,64]{1,0:T(8,128)S(1)}, f32[512]{0:T(512)S(1)}, f32[32,64,512]{2,1,0:T(8,128)S(1)}) fusion(f32[32,64,512]{2,1,0:T(8,128)} %bitcast.101, f32[32,64]{1,0:T(8,128)S(1)} %copy-done.14, f32[32,64]{1,0:T(8,128)S(1)} %copy-done.15, f32[512]{0:T(512)S(1)} %copy-done.16, ...), kind=kOutput, calls=%fused_computation.23 | convolution fusion | flops 3230657536 | bytes 16291840 | tf_op jit(solution)/shard_map/dot_general | solution.py:28
  425.3 4.3 all-to-all-start.2
  430.0 8.6 %fusion.31 = f32[512,1536]{1,0:T(8,128)} fusion(bf16[2048,512]{1,0:T(8,128)(2,1)} %bitcast.109, bf16[2048,1536]{0,1:T(8,128)(2,1)} %convert_element_type.88), kind=kOutput, calls=%fused_computation.67 | convolution fusion | flops 3221225472 | bytes 11534336 | tf_op jit(solution)/shard_map/dot_general | solution.py:22
  438.6 19.8 %all-to-all-done.2 = bf16[1,8,4,1,16,4,512]{6,5,4,2,3,0,1:T(4,128)(2,1)} async-done(((bf16[1,8,4,1,16,4,512]{6,5,4,2,3,0,1:T(4,128)(2,1)}), bf16[1,8,4,1,16,4,512]{6,5,4,2,3,0,1:T(4,128)(2,1)}, u32[]{:S(2)}, u32[]{:S(2)}) %all-to-all-start.2) | async-done | bytes 2097184 | tf_op jit(solution)/shard_map/all_to_all | solution.py:125
  458.4 5.1 copy.156
  463.5 13.1 %all-to-all-start.3 = ((bf16[1,8,4,1,16,4,512]{6,1,5,2,3,0,4:T(8,128)(2,1)}), bf16[1,8,4,1,16,4,512]{6,1,5,2,3,0,4:T(8,128)(2,1)}, u32[]{:S(2)}, u32[]{:S(2)}) async-start(bf16[1,8,4,1,16,4,512]{6,1,5,2,3,0,4:T(8,128)(2,1)} %copy.156), calls=%async_computation.3 | async-start | bytes 4194304 | tf_op jit(solution)/shard_map/all_to_all | solution.py:124
  476.6 88.2 %all-reduce = (f32[512]{0:T(512)S(1)}, f32[512]{0:T(512)S(1)}) all-reduce(f32[512]{0:T(512)S(1)} %get-tuple-element.5, f32[512]{0:T(512)S(1)} %get-tuple-element.8), channel_id=1, replica_groups=mesh['gx'=8,'gy'=16] {'gx','gy'}, use_global_device_ids=true, to_apply=%region_10.11 | all-reduce | flops 1024 | bytes 8192 | tf_op jit(solution)/shard_map/psum | solution.py:117
  566.0 54.6 %all-reduce.4.cloned.1.call-done = (f32[512,1536]{1,0:T(8,128)}, f32[512,512]{1,0:T(8,128)}) async-done(((f32[512,1536]{1,0:T(8,128)}, f32[512,512]{1,0:T(8,128)}), (f32[512,1536]{1,0:T(8,128)}, f32[512,512]{1,0:T(8,128)})) %all-reduce.4.cloned.1.call-update) | async-done | bytes 4194320 | tf_op jit(solution)/shard_map/psum | solution.py:117
  622.9 3.8 broadcast_multiply_fusion
  626.7 4.0 copy.157
  630.7 4.0 reshape.223
  (70 shorter events, 21.7 us)
Async XLA Ops:
  7.2 184.4 %copy-start = (bf16[512,1536]{1,0:T(8,128)(2,1)S(1)}, bf16[512,1536]{1,0:T(8,128)(2,1)}, u32[]{:S(2)}) copy-start(bf16[512,1536]{1,0:T(8,128)(2,1)} %param.11) | copy-start | bytes 4718596
  86.0 7.5 %copy-start.19 = (f32[16,225]{1,0:T(8,128)S(1)}, f32[16,225]{1,0:T(8,128)}, u32[]{:S(2)}) copy-start(f32[16,225]{1,0:T(8,128)} %param.13) | copy-start | bytes 43204
  86.0 59.9 %all-to-all-start.1 = ((bf16[2,1,8,4,1,16,4,512]{7,6,3,2,4,1,0,5:T(4,128)(2,1)}), bf16[2,1,8,4,1,16,4,512]{7,6,3,2,4,1,0,5:T(4,128)(2,1)}, u32[]{:S(2)}, u32[]{:S(2)}) async-start(bf16[2,1,8,4,1,16,4,512]{7,6,3,2,4,1,0,5:T(4,128)(2,1)} %copy.132), calls=%async_computation.1 | async-start | bytes 8388608 | tf_op jit(solution)/shard_map/all_to_all | solution.py:103
  152.6 1.9 copy-start.2
  156.0 9.9 %copy-start.11 = (f32[4,2,4,8,8]{3,2,1,4,0:T(4,128)}, f32[4,2,4,8,8]{3,2,1,4,0:T(4,128)S(1)}, u32[]{:S(2)}) copy-start(f32[4,2,4,8,8]{3,2,1,4,0:T(4,128)S(1)} %copy.136) | copy-start | bytes 24580
  172.1 3.2 copy-start.18
  174.0 1.3 copy-start.10
  181.8 7.1 %copy-start.16 = (f32[512]{0:T(512)S(1)}, f32[512]{0:T(512)}, u32[]{:S(2)}) copy-start(f32[512]{0:T(512)} %param.9) | copy-start | bytes 6148
  181.8 7.1 %copy-start.17 = (f32[512]{0:T(512)S(1)}, f32[512]{0:T(512)}, u32[]{:S(2)}) copy-start(f32[512]{0:T(512)} %param.10) | copy-start | bytes 6148
  232.2 1.9 copy-start.1
  333.5 9.7 %copy-start.7 = (bf16[32,64,1,16,32]{1,4,3,0,2:T(8,128)(2,1)S(1)}, bf16[32,64,1,16,32]{1,4,3,0,2:T(8,128)(2,1)}, u32[]{:S(2)}) copy-start(bf16[32,64,1,16,32]{1,4,3,0,2:T(8,128)(2,1)} %multiply_bitcast_fusion) | copy-start | bytes 6291460
  333.5 9.7 %copy-start.9 = (bf16[32,64,1,16,32]{1,4,3,0,2:T(8,128)(2,1)S(1)}, bf16[32,64,1,16,32]{1,4,3,0,2:T(8,128)(2,1)}, u32[]{:S(2)}) copy-start(bf16[32,64,1,16,32]{1,4,3,0,2:T(8,128)(2,1)} %fusion.18) | copy-start | bytes 6291460
  356.9 5.9 copy-start.3
  356.9 5.9 copy-start.12
  356.9 5.9 copy-start.13
  362.8 4.2 copy-start.5
  367.0 5.8 copy-start.8
  388.8 17.9 %copy-start.14 = (f32[32,64]{1,0:T(8,128)S(1)}, f32[32,64]{1,0:T(8,128)}, u32[]{:S(2)}) copy-start(f32[32,64]{1,0:T(8,128)} %div.40) | copy-start | bytes 24580
  388.8 17.9 %copy-start.15 = (f32[32,64]{1,0:T(8,128)S(1)}, f32[32,64]{1,0:T(8,128)}, u32[]{:S(2)}) copy-start(f32[32,64]{1,0:T(8,128)} %rsqrt.17) | copy-start | bytes 24580
  406.7 13.8 %copy-start.4 = (f32[1,1,4,2,4,8,8,512]{7,6,5,4,3,2,1,0:T(8,128)S(1)}, f32[1,1,4,2,4,8,8,512]{7,6,5,4,3,2,1,0:T(8,128)}, u32[]{:S(2)}) copy-start(f32[1,1,4,2,4,8,8,512]{7,6,5,4,3,2,1,0:T(8,128)} %copy.138) | copy-start | bytes 12582916
  406.8 13.8 %copy-start.6 = (f32[1,1,4,2,4,8,8,512]{7,6,5,4,3,2,1,0:T(8,128)S(1)}, f32[1,1,4,2,4,8,8,512]{7,6,5,4,3,2,1,0:T(8,128)}, u32[]{:S(2)}) copy-start(f32[1,1,4,2,4,8,8,512]{7,6,5,4,3,2,1,0:T(8,128)} %copy.134) | copy-start | bytes 12582916
  425.3 33.1 %all-to-all-start.2 = ((bf16[1,8,4,1,16,4,512]{6,5,4,2,3,0,1:T(4,128)(2,1)}), bf16[1,8,4,1,16,4,512]{6,5,4,2,3,0,1:T(4,128)(2,1)}, u32[]{:S(2)}, u32[]{:S(2)}) async-start(bf16[1,8,4,1,16,4,512]{6,5,4,2,3,0,1:T(4,128)(2,1)} %copy.155), calls=%async_computation.2 | async-start | bytes 4194304 | tf_op jit(solution)/shard_map/all_to_all | solution.py:125
  429.7 190.9 %all-reduce.4.cloned.1.call-start = ((), (), s32[]{:S(2)}) async-start(), calls=%async_computation.4 | async-start | bytes 8388608 | tf_op jit(solution)/shard_map/psum | solution.py:117
  463.5 163.2 %all-to-all-start.3 = ((bf16[1,8,4,1,16,4,512]{6,1,5,2,3,0,4:T(8,128)(2,1)}), bf16[1,8,4,1,16,4,512]{6,1,5,2,3,0,4:T(8,128)(2,1)}, u32[]{:S(2)}, u32[]{:S(2)}) async-start(bf16[1,8,4,1,16,4,512]{6,1,5,2,3,0,4:T(8,128)(2,1)} %copy.156), calls=%async_computation.3 | async-start | bytes 4194304 | tf_op jit(solution)/shard_map/all_to_all | solution.py:124
Sparse Core Ops, SparseCore 0:
  438.7 181.8 all-reduce.3
where the time goes:
time: 650 us; the launch traced here: 642 us
  local copies, waits for them, and re-layouts  156 us (24%)
  blocking collectives  146 us (22%)
  waiting for transfers between devices  125 us (19%)
  matrix products  112 us (17%)
  other arithmetic  63.2 us (10%)
  starting transfers between devices  25.1 us (4%)
  between operations  14.8 us (2%)
    psum x1, blocking collectives, body(): lax.psum((grad_qkv, grad_out, gain_gradient, grad_bias), ('gx', 'gy'))  88.2 us
    all_to_all x1, blocking collectives, body(): lax.all_to_all(stacked, 'gx', split_axis=2, concat_axis=2, tiled=True)  58 us
    psum x1, waiting for transfers between devices, body(): lax.psum((grad_qkv, grad_out, gain_gradient, grad_bias), ('gx', 'gy'))  54.6 us
    all_to_all x1, waiting for transfers between devices, body(): lax.all_to_all(lax.all_to_all(stacked, 'gx', split_axis=2, concat_axis=2,...  50.6 us
    convert_element_type x3, local copies, waits for them, and re-layouts, window_backward(): jnp.stack([d_query, d_keys, d_vals], axis=2).astype(jnp.bfloat16)  34 us
    all_to_all x1, waiting for transfers between devices, body(): lax.all_to_all(sending, 'gx', split_axis=1, concat_axis=1, tiled=True)  19.8 us
    reshape x1, local copies, waits for them, and re-layouts, window_backward(): qkv = qkv.reshape(count, 64, 3, heads, head_dim)  18.6 us
    sub x1, other arithmetic, window_backward(): probs = jnp.exp(scores - highest)  17.8 us
  transfers between devices with their start and end apart: 4, of which 3 were waited for; matrix products, arithmetic and copies ran while one was open for 4% of the time, Pallas kernels for 0%

commit v1 on v0

v1 whole, which is shorter than its diff:
```python
import math

import jax
import jax.numpy as jnp
from jax import lax
from jax.experimental import pallas as pl
from jax.experimental.pallas import tpu as pltpu
from jax.sharding import Mesh, PartitionSpec as P

F32 = jnp.float32
BF16 = jnp.bfloat16
HEADS = 16
CELLS = 64
PARTS = 2
STEP = 4
ROWS = STEP * CELLS
GROUPS = 4
FACTOR = 1.0 / math.sqrt(32.0)
NATURAL = (0, 1, 2, 3)
SWAPPED = (0, 2, 1, 3)
MIB = 1 << 20


def dot(left, right):
    return jnp.dot(left, right, preferred_element_type=F32)


def dot_cols(left, right):
    return lax.dot_general(left, right, (((1,), (1,)), ((), ())), preferred_element_type=F32)


def dot_rows(left, right):
    return lax.dot_general(left, right, (((0,), (0,)), ((), ())), preferred_element_type=F32)


def spread(block, mask_ref, order):
    return jnp.concatenate([block * mask_ref[h] for h in order], axis=0)


def turn(block):
    tall = jnp.concatenate([block[:, :128], block[:, 128:]], axis=0)
    tall = tall.T
    return jnp.concatenate([tall[:64], tall[64:]], axis=1)


def scatter_rows(source_ref, slab):
    windows = source_ref.shape[1]

    def fill(n, carry):
        rows = pl.ds(pl.multiple_of(n * windows, windows), windows)
        for k in range(4):
            slab[k, rows, :] = source_ref[n, :, k * 128 : k * 128 + 128].astype(F32)
        return carry

    lax.fori_loop(0, CELLS, fill, 0)


def window_rows(slab, first, windows):
    return jnp.concatenate(
        [
            jnp.concatenate(
                [slab[k, pl.ds(first + j, CELLS, stride=windows), :] for j in range(STEP)], axis=0
            )
            for k in range(4)
        ],
        axis=1,
    )


def standardise(values):
    centred = values - jnp.mean(values, -1, keepdims=True)
    variance = jnp.mean(centred * centred, -1, keepdims=True)
    inverse = lax.rsqrt(variance + 1e-05)
    return centred * inverse, inverse


def forward_kernel(
    x_ref, gain_ref, shift_ref, wqkv_ref, bias_ref, mask_ref,
    xw_ref, qkv_ref, probs_ref, att_ref, slab
):
    windows = x_ref.shape[1]
    step = pl.program_id(0)

    @pl.when(step == 0)
    def _():
        scatter_rows(x_ref, slab)

    values = window_rows(slab, step * STEP, windows)
    xw_ref[...] = values.astype(BF16)
    xhat, _ = standardise(values)
    normed = (xhat * gain_ref[...] + shift_ref[...]).astype(BF16)
    qkv_ref[...] = dot(normed, wqkv_ref[...]).astype(BF16)
    for j in range(STEP):
        rows = pl.ds(j * CELLS, CELLS)
        for g in range(GROUPS):
            q4 = qkv_ref[rows, g * 128 : g * 128 + 128]
            k4 = qkv_ref[rows, 512 + g * 128 : 512 + g * 128 + 128]
            v4 = qkv_ref[rows, 1024 + g * 128 : 1024 + g * 128 + 128]
            scores = dot_cols(k4, spread(q4, mask_ref, NATURAL)) * FACTOR + bias_ref[g]
            probs = jnp.exp(scores - jnp.max(scores, 0, keepdims=True))
            probs = probs * (1.0 / jnp.sum(probs, 0, keepdims=True))
            probs = probs.astype(BF16)
            probs_ref[pl.ds((j * GROUPS + g) * CELLS, CELLS), :] = probs
            att_ref[rows, g * 128 : g * 128 + 128] = dot(
                turn(probs), spread(v4, mask_ref, SWAPPED)
            ).astype(BF16)


def backward_kernel(
    cot_ref, xw_ref, qkv_ref, probs_ref, att_ref, gain_ref, shift_ref, wqkv_ref, wout_ref, mask_ref,
    *refs, first
):
    if first:
        out_ref, gq_ref, go_ref, ln_ref, slab, result, dqkv = refs
    else:
        gq_in, go_in, ln_in, out_ref, gq_ref, go_ref, ln_ref, slab, result, dqkv = refs
    windows = cot_ref.shape[1]
    step = pl.program_id(0)

    @pl.when(step == 0)
    def _():
        scatter_rows(cot_ref, slab)
        if first:
            gq_ref[...] = jnp.zeros_like(gq_ref)
            go_ref[...] = jnp.zeros_like(go_ref)
            ln_ref[...] = jnp.zeros_like(ln_ref)
        else:
            gq_ref[...] = gq_in[...]
            go_ref[...] = go_in[...]
            ln_ref[...] = ln_in[...]

    cot = window_rows(slab, step * STEP, windows)
    cot_b = cot.astype(BF16)
    d_att = dot_cols(cot_b, wout_ref[...]).astype(BF16)
    for j in range(STEP):
        rows = pl.ds(j * CELLS, CELLS)
        for g in range(GROUPS):
            lanes = slice(g * 128, g * 128 + 128)
            q4 = qkv_ref[rows, g * 128 : g * 128 + 128]
            k4 = qkv_ref[rows, 512 + g * 128 : 512 + g * 128 + 128]
            v4 = qkv_ref[rows, 1024 + g * 128 : 1024 + g * 128 + 128]
            d_att_bd = spread(d_att[j * CELLS : j * CELLS + CELLS, lanes], mask_ref, NATURAL)
            probs_b = probs_ref[pl.ds((j * GROUPS + g) * CELLS, CELLS), :]
            probs = probs_b.astype(F32)
            d_probs = dot_cols(v4, d_att_bd)
            d_scores = probs * (d_probs - jnp.sum(probs * d_probs, 0, keepdims=True))
            ds_b = d_scores.astype(BF16)
            d_vals = dot(probs_b, d_att_bd)
            d_keys = dot(ds_b, spread(q4, mask_ref, NATURAL)) * FACTOR
            d_query = dot(turn(ds_b), spread(k4, mask_ref, SWAPPED)) * FACTOR
            dqkv[rows, g * 128 : g * 128 + 128] = d_query.astype(BF16)
            dqkv[rows, 512 + g * 128 : 512 + g * 128 + 128] = d_keys.astype(BF16)
            dqkv[rows, 1024 + g * 128 : 1024 + g * 128 + 128] = d_vals.astype(BF16)
    go_ref[...] += dot_rows(att_ref[...], cot_b)
    xhat, inverse = standardise(xw_ref[...].astype(F32))
    normed = (xhat * gain_ref[...] + shift_ref[...]).astype(BF16)
    d_qkv = dqkv[...]
    gq_ref[...] += dot_rows(normed, d_qkv)
    d_normed = dot_cols(d_qkv, wqkv_ref[...])
    weighted = xhat * d_normed
    ln_ref[0] += jnp.sum(weighted.reshape(ROWS // 8, 8, 512), 0)
    ln_ref[1] += jnp.sum(d_normed.reshape(ROWS // 8, 8, 512), 0)
    d_hat = d_normed * gain_ref[...]
    value = cot + inverse * (
        d_hat
        - jnp.mean(d_hat, -1, keepdims=True)
        - xhat * jnp.mean(d_hat * xhat, -1, keepdims=True)
    )
    for j in range(STEP):
        for k in range(4):
            result[k, pl.ds(step * STEP + j, CELLS, stride=windows), :] = value[
                j * CELLS : j * CELLS + CELLS, k * 128 : k * 128 + 128
            ]

    @pl.when(step == pl.num_programs(0) - 1)
    def _():
        def empty(n, carry):
            rows = pl.ds(pl.multiple_of(n * windows, windows), windows)
            for k in range(4):
                out_ref[n, :, k * 128 : k * 128 + 128] = result[k, rows, :].astype(BF16)
            return carry

        lax.fori_loop(0, CELLS, empty, 0)


def whole(shape):
    return pl.BlockSpec(shape, lambda i: (0,) * len(shape))


def rows_spec(rows, width, offset=0):
    return pl.BlockSpec((rows, width), lambda i: (i + offset, 0))


def forward(x, gain, shift, w_qkv, bias, mask):
    windows = x.shape[1]
    cells = windows * CELLS
    return pl.pallas_call(
        forward_kernel,
        grid=(windows // STEP,),
        in_specs=[
            whole(x.shape), whole(gain.shape), whole(shift.shape), whole(w_qkv.shape),
            whole(bias.shape), whole(mask.shape),
        ],
        out_specs=[
            rows_spec(ROWS, 512), rows_spec(ROWS, 1536),
            rows_spec(ROWS * GROUPS, 256), rows_spec(ROWS, 512),
        ],
        out_shape=[
            jax.ShapeDtypeStruct((cells, 512), BF16),
            jax.ShapeDtypeStruct((cells, 1536), BF16),
            jax.ShapeDtypeStruct((cells * GROUPS, 256), BF16),
            jax.ShapeDtypeStruct((cells, 512), BF16),
        ],
        scratch_shapes=[pltpu.VMEM((4, cells, 128), F32)],
        compiler_params=pltpu.CompilerParams(vmem_limit_bytes=40 * MIB),
        cost_estimate=pl.CostEstimate(
            flops=15 * 10**9, bytes_accessed=20 * MIB, transcendentals=2 * 10**6
        ),
        name="window_forward",
    )(x, gain, shift, w_qkv, bias, mask)


def backward(part, cot, saved, gain, shift, w_qkv, w_out, mask, sums):
    windows = cot.shape[1]
    steps = windows // STEP
    xw, qkv, probs, att = saved
    off = part * steps
    grads = [
        jax.ShapeDtypeStruct((512, 1536), F32),
        jax.ShapeDtypeStruct((512, 512), F32),
        jax.ShapeDtypeStruct((2, 8, 512), F32),
    ]

    def kernel(*refs):
        backward_kernel(*refs, first=sums is None)

    return pl.pallas_call(
        kernel,
        grid=(steps,),
        in_specs=[
            whole(cot.shape),
            rows_spec(ROWS, 512, off), rows_spec(ROWS, 1536, off),
            rows_spec(ROWS * GROUPS, 256, off), rows_spec(ROWS, 512, off),
            whole(gain.shape), whole(shift.shape), whole(w_qkv.shape), whole(w_out.shape),
            whole(mask.shape),
        ]
        + ([] if sums is None else [whole(s.shape) for s in sums]),
        out_specs=[whole(cot.shape)] + [whole(s.shape) for s in grads],
        out_shape=[jax.ShapeDtypeStruct(cot.shape, BF16)] + grads,
        scratch_shapes=[
            pltpu.VMEM((4, windows * CELLS, 128), F32),
            pltpu.VMEM((4, windows * CELLS, 128), F32),
            pltpu.VMEM((ROWS, 1536), BF16),
        ],
        compiler_params=pltpu.CompilerParams(vmem_limit_bytes=48 * MIB),
        cost_estimate=pl.CostEstimate(
            flops=15 * 10**9, bytes_accessed=20 * MIB, transcendentals=0
        ),
        name="window_backward",
    )(cot, xw, qkv, probs, att, gain, shift, w_qkv, w_out, mask, *(sums or ()))


def bias_tables(rel_bias):
    position = jnp.arange(CELLS, dtype=jnp.int32)
    prow = position // 8
    pcol = position % 8
    offset = (prow[None, :] - prow[:, None] + 7) * 15 + (pcol[None, :] - pcol[:, None] + 7)
    onehot = (offset.reshape(1, -1) == jnp.arange(225, dtype=jnp.int32)[:, None]).astype(F32)
    full = jnp.dot(rel_bias, onehot, precision=lax.Precision.HIGHEST)
    full = full.reshape(GROUPS, HEADS // GROUPS, CELLS, CELLS).transpose(0, 2, 1, 3)
    return full.reshape(GROUPS, CELLS, 256)


def after(value, *others):
    return lax.optimization_barrier((value,) + others)[0]


def exchange(array):
    return lax.all_to_all(array, ("gx", "gh"), split_axis=0, concat_axis=0, tiled=True)


def swap_cores(array):
    return lax.ppermute(array, "core", [(0, 1), (1, 0)])


def body(latent, cotangent, gain, shift, w_qkv, w_out, rel_bias):
    rows, cols, width = latent.shape
    peers = lax.axis_size("gx") * lax.axis_size("gh")
    windows = rows * cols // peers
    per_part = windows // PARTS
    norm = 1.0 / math.sqrt(rows * cols * peers * lax.axis_size("core"))
    core = lax.axis_index("core")
    gain = gain.reshape(1, width)
    shift = shift.reshape(1, width)
    lane = jnp.arange(128, dtype=jnp.int32) // 32
    mask = jnp.broadcast_to(
        (lane[None, None, :] == jnp.arange(4, dtype=jnp.int32)[:, None, None]).astype(BF16),
        (4, CELLS, 128),
    )
    bias = bias_tables(rel_bias)

    latent = latent.reshape(peers, windows, width)
    cotangent = cotangent.reshape(peers, windows, width)
    x = exchange(latent)
    previous = x
    cots = []
    for p in range(PARTS):
        piece = after(cotangent[:, p * per_part : (p + 1) * per_part], previous)
        previous = exchange(piece)
        cots.append(previous)
    saved = forward(x, gain, shift, w_qkv, bias, mask)
    sums = None
    pieces = []
    for p in range(PARTS):
        d_latent, *sums = backward(p, cots[p], saved, gain, shift, w_qkv, w_out, mask, sums)
        pieces.append(exchange(d_latent))
    grad_qkv, grad_out, ln = sums
    result = jnp.concatenate(pieces, axis=1).reshape(rows, cols, width)

    ln = jnp.sum(ln, axis=1)
    column = jnp.zeros((2, width, 128), F32).at[:, :, 0].set(ln)
    halves = jnp.stack(
        [
            jnp.concatenate([grad_qkv[:, :1024], column[0]], axis=1),
            jnp.concatenate([grad_qkv[:, 1024:], grad_out, column[1]], axis=1),
        ]
    )
    mine = lax.dynamic_index_in_dim(halves, core, 0, keepdims=False)
    other = lax.dynamic_index_in_dim(halves, 1 - core, 0, keepdims=False).astype(BF16)
    mine = (mine + swap_cores(other).astype(F32)).astype(BF16)
    parts = exchange(mine.reshape(peers, 8, 1152))
    total = (jnp.sum(parts.astype(F32), axis=0) * norm).astype(BF16)
    full = exchange(jnp.broadcast_to(total[None], parts.shape)).reshape(width, 1152)
    theirs = swap_cores(full)
    low = jnp.where(core == 0, full, theirs).astype(F32)
    high = jnp.where(core == 0, theirs, full).astype(F32)
    return (
        result,
        jnp.concatenate([low[:, :1024], high[:, :512]], axis=1),
        high[:, 512:1024],
        low[:, 1024],
        high[:, 1024],
    )


def solution(mesh):
    cores = mesh.devices.reshape(mesh.shape["gx"], mesh.shape["gy"] // 2, 2)
    inner = Mesh(cores, ("gx", "gh", "core"))
    block = P("gx", ("gh", "core"), None)
    return jax.shard_map(
        body,
        mesh=inner,
        in_specs=(block, block, P(), P(), P(), P(), P()),
        out_specs=(block, P(), P(), P(), P()),
        check_vma=False,
    )
```

time: 650 us -> 286 us (0.44)
  local copies, waits for them, and re-layouts: 156 us -> 24.9 us
  matrix products: 112 us -> 1.33 us
  blocking collectives: 146 us -> 50.9 us
  Pallas kernels: 0 us -> 93.2 us
  waiting for transfers between devices: 125 us -> 50.5 us
  other arithmetic: 63.2 us -> 11.4 us
  starting transfers between devices: 25.1 us -> 49.2 us
  between operations: 14.8 us -> 0.89 us
    dot_general x12 -> x1, matrix products: 112 us -> 1.33 us  [bias_tables(): full = jnp.dot(rel_bias, onehot, precision=lax.Precision.HIGHEST)]
    pallas_call x0 -> x3, Pallas kernels: none -> 93.2 us  [the longest x2 49.9 us: backward(): pl.pallas_call(kernel, grid=(steps,), in_specs=[whole(cot.shape), rows_sp...]
    psum x1 -> x0, blocking collectives: 88.2 us -> none  [body(): lax.psum((grad_qkv, grad_out, gain_gradient, grad_bias), ('gx', 'gy'))]
    convert_element_type x9 -> x0, local copies, waits for them, and re-layouts: 66.3 us -> none  [the longest x3 34 us: window_backward(): jnp.stack([d_query, d_keys, d_vals], axis=2).astype(jnp.bfloat16)]
    psum x1 -> x0, waiting for transfers between devices: 54.6 us -> none  [body(): lax.psum((grad_qkv, grad_out, gain_gradient, grad_bias), ('gx', 'gy'))]
    reshape x5 -> x3, local copies, waits for them, and re-layouts: 37.3 us -> 0.9 us  [the longest x2 0.56 us: bias_tables(): full.reshape(GROUPS, HEADS // GROUPS, CELLS, CELLS).transpose(0, 2, 1, 3)]
    convert_element_type x6 -> x4, other arithmetic: 29.7 us -> 3.16 us  [the longest x1 1.58 us: body(): low = jnp.where(core == 0, full, theirs).astype(F32)]
    all_to_all x3 -> x5, waiting for transfers between devices: 70.4 us -> 47.7 us  [exchange(): lax.all_to_all(array, ('gx', 'gh'), split_axis=0, concat_axis=0, tiled=True)]
  transfers between devices with their start and end apart: 4 -> 7, of which waited for: 3 -> 4; matrix products, arithmetic and copies ran while one was open for 4% -> 3% of each run, Pallas kernels for 0% -> 24%
where the time goes in v1:
time: 286 us; the launch traced here: 282 us
  Pallas kernels  93.2 us (33%)
  blocking collectives  50.9 us (18%)
  waiting for transfers between devices  50.5 us (18%)
  starting transfers between devices  49.2 us (17%)
  local copies, waits for them, and re-layouts  24.9 us (9%)
  other arithmetic  11.4 us (4%)
    all_to_all x2, blocking collectives, exchange(): lax.all_to_all(array, ('gx', 'gh'), split_axis=0, concat_axis=0, tiled=True)  50.9 us
    pallas_call x2, Pallas kernels, backward(): pl.pallas_call(kernel, grid=(steps,), in_specs=[whole(cot.shape), rows_sp...  49.9 us
    all_to_all x5, waiting for transfers between devices, exchange(): lax.all_to_all(array, ('gx', 'gh'), split_axis=0, concat_axis=0, tiled=True)  47.7 us
    pallas_call x1, Pallas kernels, forward(): pl.pallas_call(forward_kernel, grid=(windows // STEP,), in_specs=[whole(x...  43.3 us
    all_to_all x5, starting transfers between devices, exchange(): lax.all_to_all(array, ('gx', 'gh'), split_axis=0, concat_axis=0, tiled=True)  42.5 us
    unnamed x30, local copies, waits for them, and re-layouts  12.1 us
    ppermute x2, starting transfers between devices, swap_cores(): return lax.ppermute(array, 'core', [(0, 1), (1, 0)])  6.71 us
  transfers between devices with their start and end apart: 7, of which 4 were waited for; matrix products, arithmetic and copies ran while one was open for 3% of the time, Pallas kernels for 24%

profile of v1, /device:TPU:1, one launch (start us, length us, event | category | flops | bytes accessed | tf_op | source)
XLA Modules:
  0.0 282.2 jit_solution(868413504149155837)
XLA Ops:
  0.6 12.0 %all-to-all-start = ((bf16[64,32,512]{2,1,0:T(8,128)(2,1)}), bf16[64,32,512]{2,1,0:T(8,128)(2,1)S(1)}, u32[]{:S(2)}, u32[]{:S(2)}) async-start(bf16[64,32,512]{2,1,0:T(8,128)(2,1)} %bitcast.43), calls=%async_computation | async-start | bytes 4194304 | tf_op jit(solution)/shard_map/all_to_all | solution.py:279
  12.6 0.1 add_add_fusion
  12.8 1.3 convolution_bitcast_fusion
  14.1 0.2 reshape.201
  14.4 0.3 copy.16
  14.7 0.3 reshape.202.bias_ref
  15.1 3.1 %fusion.13 = (bf16[64,16,512]{2,1,0:T(8,128)(2,1)}, bf16[64,16,512]{2,1,0:T(8,128)(2,1)}) fusion(bf16[64,32,512]{2,1,0:T(8,128)(2,1)} %bitcast.42), kind=kLoop, calls=%fused_computation.43 | loop fusion | bytes 4194304 | tf_op jit(solution)/shard_map/slice | solution.py:308
  18.2 21.7 %all-to-all-done.x_ref = bf16[64,32,512]{2,1,0:T(8,128)(2,1)S(1)} async-done(((bf16[64,32,512]{2,1,0:T(8,128)(2,1)}), bf16[64,32,512]{2,1,0:T(8,128)(2,1)S(1)}, u32[]{:S(2)}, u32[]{:S(2)}) %all-to-all-start) | async-done | bytes 2097184 | tf_op jit(solution)/shard_map/all_to_all | solution.py:279
  39.9 7.8 %all-to-all-start.1 = ((bf16[64,16,512]{2,1,0:T(8,128)(2,1)}), bf16[64,16,512]{2,1,0:T(8,128)(2,1)S(1)}, u32[]{:S(2)}, u32[]{:S(2)}) async-start(bf16[64,16,512]{2,1,0:T(8,128)(2,1)} %get-tuple-element.31), calls=%async_computation.1 | async-start | bytes 2097152 | tf_op jit(solution)/shard_map/all_to_all | solution.py:279
  47.7 1.4 copy-done.2
  49.1 43.3 %window_forward.1 = (bf16[2048,512]{1,0:T(8,128)(2,1)S(1)}, bf16[2048,1536]{1,0:T(8,128)(2,1)}, bf16[8192,256]{1,0:T(8,128)(2,1)S(1)}, bf16[2048,512]{1,0:T(8,128)(2,1)S(1)}) custom-call(bf16[64,32,512]{2,1,0:T(8,128)(2,1)S(1)} %all-to-all-done.x_ref, f32[1,512]{1,0:T(1,128)S(1)} %bitcast.35, f32[1,512]{1,0:T(1,128)S(1)} %bitcast.38, ...), custom_call_target="tpu_custom_call" | custom-call | flops 15000000512 | bytes 20971520 | tf_op jit(solution)/shard_map/window_forward/pallas_call | solution.py:197
  92.4 2.1 copy-done.8
  94.5 1.3 copy-done.9
  95.8 1.3 copy-done.10
  97.1 10.0 %all-to-all-start.3 = ((bf16[64,16,512]{2,1,0:T(8,128)(2,1)}), bf16[64,16,512]{2,1,0:T(8,128)(2,1)S(1)}, u32[]{:S(2)}, u32[]{:S(2)}) async-start(bf16[64,16,512]{2,1,0:T(8,128)(2,1)} %get-tuple-element.37), calls=%async_computation.3 | async-start | bytes 2097152 | tf_op jit(solution)/shard_map/all_to_all | solution.py:279
  107.1 1.4 copy-done.3
  108.5 1.0 copy-done.4
  109.6 24.0 %window_backward.2 = (bf16[64,16,512]{2,1,0:T(8,128)(2,1)}, f32[512,1536]{1,0:T(8,128)}, f32[512,512]{1,0:T(8,128)S(1)}, f32[2,8,512]{2,1,0:T(8,128)S(1)}) custom-call(bf16[64,16,512]{2,1,0:T(8,128)(2,1)S(1)} %all-to-all-done.1.refs_0_, bf16[2048,512]{1,0:T(8,128)(2,1)} %copy-done.9, bf16[2048,1536]{1,0:T(8,128)(2,1)} %get-tuple-element.33.refs_2_, ...), custom_call_target="tpu_custom_call" | custom-call | flops 15000000512 | bytes 20971520 | tf_op jit(solution)/shard_map/window_backward/pallas_call | solution.py:237
  133.6 1.0 copy-done.11
  134.6 1.0 copy-done.5
  135.7 1.2 copy-done.12
  136.9 25.9 %window_backward.3 = (bf16[64,16,512]{2,1,0:T(8,128)(2,1)}, f32[512,1536]{1,0:T(8,128)}, f32[512,512]{1,0:T(8,128)S(1)}, f32[2,8,512]{2,1,0:T(8,128)S(1)}) custom-call(bf16[64,16,512]{2,1,0:T(8,128)(2,1)S(1)} %all-to-all-done.3.refs_0_, bf16[2048,512]{1,0:T(8,128)(2,1)} %copy-done.9, bf16[2048,1536]{1,0:T(8,128)(2,1)} %get-tuple-element.33.refs_2_, ...), custom_call_target="tpu_custom_call" | custom-call | flops 15000000512 | bytes 20971520 | tf_op jit(solution)/shard_map/window_backward/pallas_call | solution.py:237
  162.8 3.2 %slice.54 = f32[512,1024]{1,0:T(8,128)} slice(f32[512,1536]{1,0:T(8,128)} %get-tuple-element.42), slice={[0:512], [0:1024]} | slice | bytes 4194304 | tf_op jit(solution)/shard_map/slice | solution.py:324
  165.9 2.3 slice.56
  168.2 0.2 copy.14
  168.5 1.9 maximum_bitcast_fusion
  170.4 0.2 maximum_bitcast_fusion.1
  170.6 1.6 fusion.8
  172.1 0.2 copy-done.13
  172.3 3.0 %collective-permute-start = (bf16[512,1152]{1,0:T(8,128)(2,1)}, bf16[512,1152]{1,0:T(8,128)(2,1)}, u32[]{:S(2)}, u32[]{:S(2)}) collective-permute-start(bf16[512,1152]{1,0:T(8,128)(2,1)} %fusion.8), channel_id=1, source_target_pairs={{0,1},{1,0},{2,3},{3,2},{4,5},{5,4},{6,7},{7,6},{8,9},{9,8},{10,11... | collective-permute-start | bytes 3538952 | tf_op jit(solution)/shard_map/ppermute | solution.py:283
  175.4 2.8 collective-permute-done
  178.2 2.5 fusion.7
  180.6 28.5 %all_to_all.35 = bf16[64,8,1152]{2,1,0:T(8,128)(2,1)S(1)} all-to-all(bf16[64,8,1152]{2,1,0:T(8,128)(2,1)S(1)} %fusion.7), channel_id=1, replica_groups=mesh['gx'=8,'gh'=8,'core'=2] {'gx','gh'}, dimensions={0} | all-to-all | bytes 2359296 | tf_op jit(solution)/shard_map/all_to_all | solution.py:279
  209.2 6.3 %all-to-all-start.2 = ((bf16[64,16,512]{2,1,0:T(8,128)(2,1)}), bf16[64,16,512]{2,1,0:T(8,128)(2,1)S(1)}, u32[]{:S(2)}, u32[]{:S(2)}) async-start(bf16[64,16,512]{2,1,0:T(8,128)(2,1)} %get-tuple-element.36), calls=%async_computation.2 | async-start | bytes 2097152 | tf_op jit(solution)/shard_map/all_to_all | solution.py:279
  215.5 0.2 convert_reduce_fusion
  215.7 15.5 %all-to-all-done.2 = bf16[64,16,512]{2,1,0:T(8,128)(2,1)S(1)} async-done(((bf16[64,16,512]{2,1,0:T(8,128)(2,1)}), bf16[64,16,512]{2,1,0:T(8,128)(2,1)S(1)}, u32[]{:S(2)}, u32[]{:S(2)}) %all-to-all-start.2) | async-done | bytes 1048608 | tf_op jit(solution)/shard_map/all_to_all | solution.py:279
  231.2 0.1 broadcast_in_dim.9
  231.3 22.4 %all_to_all.36 = bf16[64,8,1152]{2,1,0:T(8,128)(2,1)S(1)} all-to-all(bf16[64,8,1152]{2,1,0:T(8,128)(2,1)S(1)} %broadcast_in_dim.9), channel_id=1, replica_groups=mesh['gx'=8,'gh'=8,'core'=2] {'gx','gh'}, dimensions={0} | all-to-all | bytes 2359296 | tf_op jit(solution)/shard_map/all_to_all | solution.py:279
  253.7 6.4 %all-to-all-start.4 = ((bf16[64,16,512]{2,1,0:T(8,128)(2,1)}), bf16[64,16,512]{2,1,0:T(8,128)(2,1)S(1)}, u32[]{:S(2)}, u32[]{:S(2)}) async-start(bf16[64,16,512]{2,1,0:T(8,128)(2,1)} %get-tuple-element.41), calls=%async_computation.4 | async-start | bytes 2097152 | tf_op jit(solution)/shard_map/all_to_all | solution.py:279
  260.1 3.7 %collective-permute-start.1 = (bf16[512,1152]{1,0:T(8,128)(2,1)S(1)}, bf16[512,1152]{1,0:T(8,128)(2,1)}, u32[]{:S(2)}, u32[]{:S(2)}) collective-permute-start(bf16[512,1152]{1,0:T(8,128)(2,1)S(1)} %bitcast.41), channel_id=1, source_target_pairs={{0,1},{1,0},{2,3},{3,2},{4,5},{5,4},{6,7},{7,6},{8,9},{9,8},{10,11... | collective-permute-start | bytes 3538952 | tf_op jit(solution)/shard_map/ppermute | solution.py:283
  263.7 10.5 %all-to-all-done.4 = bf16[64,16,512]{2,1,0:T(8,128)(2,1)S(1)} async-done(((bf16[64,16,512]{2,1,0:T(8,128)(2,1)}), bf16[64,16,512]{2,1,0:T(8,128)(2,1)S(1)}, u32[]{:S(2)}, u32[]{:S(2)}) %all-to-all-start.4) | async-done | bytes 1048608 | tf_op jit(solution)/shard_map/all_to_all | solution.py:279
  274.2 1.5 pad_maximum_fusion.1
  275.7 1.6 select_convert_fusion.1
  277.3 1.3 fusion.12
  278.6 0.7 slice_reduce_fusion
  279.3 0.3 slice.65
  279.6 0.7 slice_reduce_fusion.1
  280.3 1.9 pad_maximum_fusion
  (31 shorter events, 0.2 us)
Async XLA Ops:
  0.6 12.2 %copy-start = (f32[16,225]{1,0:T(8,128)S(1)}, f32[16,225]{1,0:T(8,128)}, u32[]{:S(2)}) copy-start(f32[16,225]{1,0:T(8,128)} %param.15) | copy-start | bytes 43204
  0.6 39.2 %all-to-all-start = ((bf16[64,32,512]{2,1,0:T(8,128)(2,1)}), bf16[64,32,512]{2,1,0:T(8,128)(2,1)S(1)}, u32[]{:S(2)}, u32[]{:S(2)}) async-start(bf16[64,32,512]{2,1,0:T(8,128)(2,1)} %bitcast.43), calls=%async_computation | async-start | bytes 4194304 | tf_op jit(solution)/shard_map/all_to_all | solution.py:279
  15.1 32.6 %copy-start.6 = (f32[512]{0:T(512)S(1)}, f32[512]{0:T(512)}, u32[]{:S(2)}) copy-start(f32[512]{0:T(512)} %param.11) | copy-start | bytes 6148
  15.1 32.6 %copy-start.7 = (f32[512]{0:T(512)S(1)}, f32[512]{0:T(512)}, u32[]{:S(2)}) copy-start(f32[512]{0:T(512)} %param.12) | copy-start | bytes 6148
  39.9 57.3 %all-to-all-start.1 = ((bf16[64,16,512]{2,1,0:T(8,128)(2,1)}), bf16[64,16,512]{2,1,0:T(8,128)(2,1)S(1)}, u32[]{:S(2)}, u32[]{:S(2)}) async-start(bf16[64,16,512]{2,1,0:T(8,128)(2,1)} %get-tuple-element.31), calls=%async_computation.1 | async-start | bytes 2097152 | tf_op jit(solution)/shard_map/all_to_all | solution.py:279
  47.7 1.4 copy-start.2
  92.4 2.1 copy-start.8
  94.5 1.3 copy-start.9
  95.8 1.3 copy-start.10
  97.1 37.5 %all-to-all-start.3 = ((bf16[64,16,512]{2,1,0:T(8,128)(2,1)}), bf16[64,16,512]{2,1,0:T(8,128)(2,1)S(1)}, u32[]{:S(2)}, u32[]{:S(2)}) async-start(bf16[64,16,512]{2,1,0:T(8,128)(2,1)} %get-tuple-element.37), calls=%async_computation.3 | async-start | bytes 2097152 | tf_op jit(solution)/shard_map/all_to_all | solution.py:279
  107.1 1.4 copy-start.3
  108.5 1.0 copy-start.4
  133.6 1.0 copy-start.11
  134.6 1.0 copy-start.5
  135.7 1.2 copy-start.12
  168.5 1.9 copy-start.14
  170.5 1.8 copy-start.13
  172.3 5.8 %collective-permute-start = (bf16[512,1152]{1,0:T(8,128)(2,1)}, bf16[512,1152]{1,0:T(8,128)(2,1)}, u32[]{:S(2)}, u32[]{:S(2)}) collective-permute-start(bf16[512,1152]{1,0:T(8,128)(2,1)} %fusion.8), channel_id=1, source_target_pairs={{0,1},{1,0},{2,3},{3,2},{4,5},{5,4},{6,7},{7,6},{8,9},{9,8},{10,11... | collective-permute-start | bytes 3538952 | tf_op jit(solution)/shard_map/ppermute | solution.py:283
  209.2 22.0 %all-to-all-start.2 = ((bf16[64,16,512]{2,1,0:T(8,128)(2,1)}), bf16[64,16,512]{2,1,0:T(8,128)(2,1)S(1)}, u32[]{:S(2)}, u32[]{:S(2)}) async-start(bf16[64,16,512]{2,1,0:T(8,128)(2,1)} %get-tuple-element.36), calls=%async_computation.2 | async-start | bytes 2097152 | tf_op jit(solution)/shard_map/all_to_all | solution.py:279
  253.7 20.6 %all-to-all-start.4 = ((bf16[64,16,512]{2,1,0:T(8,128)(2,1)}), bf16[64,16,512]{2,1,0:T(8,128)(2,1)S(1)}, u32[]{:S(2)}, u32[]{:S(2)}) async-start(bf16[64,16,512]{2,1,0:T(8,128)(2,1)} %get-tuple-element.41), calls=%async_computation.4 | async-start | bytes 2097152 | tf_op jit(solution)/shard_map/all_to_all | solution.py:279
  260.1 15.7 %collective-permute-start.1 = (bf16[512,1152]{1,0:T(8,128)(2,1)S(1)}, bf16[512,1152]{1,0:T(8,128)(2,1)}, u32[]{:S(2)}, u32[]{:S(2)}) collective-permute-start(bf16[512,1152]{1,0:T(8,128)(2,1)S(1)} %bitcast.41), channel_id=1, source_target_pairs={{0,1},{1,0},{2,3},{3,2},{4,5},{5,4},{6,7},{7,6},{8,9},{9,8},{10,11... | collective-permute-start | bytes 3538952 | tf_op jit(solution)/shard_map/ppermute | solution.py:283
  280.3 1.9 copy-start.1

commit v2 on v1

v2 whole, which is shorter than its diff:
```python
import math

import jax
import jax.numpy as jnp
from jax import lax
from jax.experimental import pallas as pl
from jax.experimental.pallas import tpu as pltpu
from jax.sharding import Mesh, PartitionSpec as P

F32 = jnp.float32
BF16 = jnp.bfloat16
HEADS = 16
CELLS = 64
PARTS = 2
STEP = 4
ROWS = STEP * CELLS
GROUPS = 4
FACTOR = 1.0 / math.sqrt(32.0)
NATURAL = (0, 1, 2, 3)
SWAPPED = (0, 2, 1, 3)
SKEW = 1
MIB = 1 << 20


def dot(left, right):
    return jnp.dot(left, right, preferred_element_type=F32)


def dot_cols(left, right):
    return lax.dot_general(left, right, (((1,), (1,)), ((), ())), preferred_element_type=F32)


def dot_rows(left, right):
    return lax.dot_general(left, right, (((0,), (0,)), ((), ())), preferred_element_type=F32)


def spread(block, mask_ref, order):
    return jnp.concatenate([block * mask_ref[h] for h in order], axis=0)


def turn(block):
    tall = jnp.concatenate([block[:, :128], block[:, 128:]], axis=0)
    tall = tall.T
    return jnp.concatenate([tall[:64], tall[64:]], axis=1)


def window_rows(slab, first, windows):
    return jnp.concatenate(
        [
            jnp.concatenate(
                [slab[k, pl.ds(first + j, CELLS, stride=windows), :] for j in range(STEP)], axis=0
            )
            for k in range(4)
        ],
        axis=1,
    )


def standardise(values):
    centred = values - jnp.mean(values, -1, keepdims=True)
    variance = jnp.mean(centred * centred, -1, keepdims=True)
    inverse = lax.rsqrt(variance + 1e-05)
    return centred * inverse, inverse


def unit(j, g, qkv, d_att, d_qkv, att, bias_ref, mask_ref):
    rows = pl.ds(j * CELLS, CELLS)
    lane = g * 128
    q4 = qkv[rows, lane : lane + 128]
    k4 = qkv[rows, 512 + lane : 512 + lane + 128]
    v4 = qkv[rows, 1024 + lane : 1024 + lane + 128]
    q_wide = spread(q4, mask_ref, NATURAL)
    d_att_wide = spread(d_att[rows, lane : lane + 128], mask_ref, NATURAL)
    scores = dot_cols(k4, q_wide) * FACTOR + bias_ref[g]
    d_probs = dot_cols(v4, d_att_wide)
    yield
    probs = jnp.exp(scores - jnp.max(scores, 0, keepdims=True))
    probs = probs * (1.0 / jnp.sum(probs, 0, keepdims=True))
    probs_b = probs.astype(BF16)
    d_scores = probs * (d_probs - jnp.sum(probs * d_probs, 0, keepdims=True))
    ds_b = d_scores.astype(BF16)
    yield
    turned = turn(probs_b)
    ds_turned = turn(ds_b)
    yield
    attended = dot(turned, spread(v4, mask_ref, SWAPPED))
    d_query = dot(ds_turned, spread(k4, mask_ref, SWAPPED)) * FACTOR
    d_keys = dot(ds_b, q_wide) * FACTOR
    d_vals = dot(probs_b, d_att_wide)
    att[rows, lane : lane + 128] = attended.astype(BF16)
    d_qkv[rows, lane : lane + 128] = d_query.astype(BF16)
    d_qkv[rows, 512 + lane : 512 + lane + 128] = d_keys.astype(BF16)
    d_qkv[rows, 1024 + lane : 1024 + lane + 128] = d_vals.astype(BF16)


def interleave(units, skew):
    running = []
    time = 0
    units = list(units)
    while units or running:
        if units and time % skew == 0:
            running.append(units.pop(0))
        running = [u for u in running if next(u, True) is not True]
        time += 1


def window_kernel(
    core_ref, x_ref, gain_ref, shift_ref, wqkv_ref, wout_ref, bias_ref, mask_ref, *refs, last
):
    if last:
        gw_in, ln_in, out_ref, mine_ref, other_ref, ln_ref = refs[:6]
        lat_slab, cot_slab, qkv, d_att, d_qkv, att, gw_ref = refs[6:]
    else:
        out_ref, gw_ref, ln_ref = refs[:3]
        lat_slab, cot_slab, qkv, d_att, d_qkv, att = refs[3:]
    windows = x_ref.shape[1] // 2
    step = pl.program_id(0)

    @pl.when(step == 0)
    def _():
        def fill(n, carry):
            rows = pl.ds(pl.multiple_of(n * windows, windows), windows)
            for k in range(4):
                lanes = slice(k * 128, k * 128 + 128)
                lat_slab[k, rows, :] = x_ref[n, :windows, lanes].astype(F32)
                cot_slab[k, rows, :] = x_ref[n, windows:, lanes].astype(F32)
            return carry

        lax.fori_loop(0, CELLS, fill, 0)
        if last:
            gw_ref[...] = gw_in[...]
            ln_ref[...] = ln_in[...]
        else:
            gw_ref[...] = jnp.zeros_like(gw_ref)
            ln_ref[...] = jnp.zeros_like(ln_ref)

    cot = window_rows(cot_slab, step * STEP, windows)
    cot_b = cot.astype(BF16)
    d_att[...] = dot_cols(cot_b, wout_ref[...]).astype(BF16)
    xhat, inverse = standardise(window_rows(lat_slab, step * STEP, windows))
    normed = (xhat * gain_ref[...] + shift_ref[...]).astype(BF16)
    qkv[...] = dot(normed, wqkv_ref[...]).astype(BF16)
    interleave(
        (
            unit(j, g, qkv, d_att, d_qkv, att, bias_ref, mask_ref)
            for j in range(STEP)
            for g in range(GROUPS)
        ),
        SKEW,
    )
    for k in range(3):
        gw_ref[k] += dot_rows(normed, d_qkv[:, k * 512 : k * 512 + 512])
    gw_ref[3] += dot_rows(att[...], cot_b)
    d_normed = dot_cols(d_qkv[...], wqkv_ref[...])
    weighted = xhat * d_normed
    ln_ref[0] += jnp.sum(weighted.reshape(ROWS // 8, 8, 512), 0)
    ln_ref[1] += jnp.sum(d_normed.reshape(ROWS // 8, 8, 512), 0)
    d_hat = d_normed * gain_ref[...]
    value = cot + inverse * (
        d_hat
        - jnp.mean(d_hat, -1, keepdims=True)
        - xhat * jnp.mean(d_hat * xhat, -1, keepdims=True)
    )
    for j in range(STEP):
        for k in range(4):
            lat_slab[k, pl.ds(step * STEP + j, CELLS, stride=windows), :] = value[
                j * CELLS : j * CELLS + CELLS, k * 128 : k * 128 + 128
            ]

    @pl.when(step == pl.num_programs(0) - 1)
    def _():
        def empty(n, carry):
            rows = pl.ds(pl.multiple_of(n * windows, windows), windows)
            for k in range(4):
                out_ref[n, :, k * 128 : k * 128 + 128] = lat_slab[k, rows, :].astype(BF16)
            return carry

        lax.fori_loop(0, CELLS, empty, 0)
        if last:
            core = core_ref[0]
            for k in range(2):
                mine_ref[k] = gw_ref[2 * core + k]
                other_ref[k] = gw_ref[2 * (1 - core) + k].astype(BF16)


def whole(shape):
    return pl.BlockSpec(shape, lambda i: (0,) * len(shape))


def window_pass(core, x, gain, shift, w_qkv, w_out, bias, mask, sums):
    last = sums is not None
    windows = x.shape[1] // 2
    cells = windows * CELLS
    shape = jax.ShapeDtypeStruct
    outs = [shape((CELLS, windows, 512), BF16)]
    if last:
        outs += [shape((2, 512, 512), F32), shape((2, 512, 512), BF16)]
    else:
        outs += [shape((4, 512, 512), F32)]
    outs += [shape((2, 8, 512), F32)]
    operands = (x, gain, shift, w_qkv, w_out, bias, mask) + tuple(sums or ())

    def kernel(*refs):
        window_kernel(*refs, last=last)

    return pl.pallas_call(
        kernel,
        grid=(windows // STEP,),
        in_specs=[pl.BlockSpec(memory_space=pltpu.SMEM)] + [whole(o.shape) for o in operands],
        out_specs=[whole(o.shape) for o in outs],
        out_shape=outs,
        scratch_shapes=[
            pltpu.VMEM((4, cells, 128), F32),
            pltpu.VMEM((4, cells, 128), F32),
            pltpu.VMEM((ROWS, 1536), BF16),
            pltpu.VMEM((ROWS, 512), BF16),
            pltpu.VMEM((ROWS, 1536), BF16),
            pltpu.VMEM((ROWS, 512), BF16),
        ]
        + ([pltpu.VMEM((4, 512, 512), F32)] if last else []),
        compiler_params=pltpu.CompilerParams(vmem_limit_bytes=52 * MIB),
        cost_estimate=pl.CostEstimate(
            flops=25 * 10**9, bytes_accessed=20 * MIB, transcendentals=10**6
        ),
        name="window_last" if last else "window_first",
    )(core, *operands)


def bias_tables(rel_bias):
    position = jnp.arange(CELLS, dtype=jnp.int32)
    prow = position // 8
    pcol = position % 8
    offset = (prow[None, :] - prow[:, None] + 7) * 15 + (pcol[None, :] - pcol[:, None] + 7)
    onehot = (offset.reshape(1, -1) == jnp.arange(225, dtype=jnp.int32)[:, None]).astype(F32)
    full = jnp.dot(rel_bias, onehot, precision=lax.Precision.HIGHEST)
    full = full.reshape(GROUPS, HEADS // GROUPS, CELLS, CELLS).transpose(0, 2, 1, 3)
    return full.reshape(GROUPS, CELLS, 256)


def after(value, *others):
    return lax.optimization_barrier((value,) + others)[0]


def exchange(array):
    return lax.all_to_all(array, ("gx", "gh"), split_axis=0, concat_axis=0, tiled=True)


def swap_cores(array):
    return lax.ppermute(array, "core", [(0, 1), (1, 0)])


def body(latent, cotangent, gain, shift, w_qkv, w_out, rel_bias):
    rows, cols, width = latent.shape
    peers = lax.axis_size("gx") * lax.axis_size("gh")
    windows = rows * cols // peers
    half = windows // PARTS
    norm = 1.0 / math.sqrt(rows * cols * peers * lax.axis_size("core"))
    core = lax.axis_index("core")
    gain = gain.reshape(1, width)
    shift = shift.reshape(1, width)
    lane = jnp.arange(128, dtype=jnp.int32) // 32
    mask = jnp.broadcast_to(
        (lane[None, None, :] == jnp.arange(4, dtype=jnp.int32)[:, None, None]).astype(BF16),
        (4, CELLS, 128),
    )
    bias = bias_tables(rel_bias)
    consts = (gain, shift, w_qkv, w_out, bias, mask)
    core_id = core.astype(jnp.int32).reshape(1)

    latent = latent.reshape(peers, windows, width)
    cotangent = cotangent.reshape(peers, windows, width)
    first = jnp.concatenate([latent[:, :half], cotangent[:, :half]], axis=1)
    second = jnp.concatenate([latent[:, half:], cotangent[:, half:]], axis=1)
    x_first = exchange(first)
    x_second = exchange(after(second, x_first))
    d_first, gw, ln = window_pass(core_id, x_first, *consts, None)
    back_first = exchange(d_first)
    d_second, mine, other, ln = window_pass(core_id, x_second, *consts, (gw, ln))

    ln = jnp.sum(ln, axis=1).reshape(8, 128)
    received = swap_cores(other).astype(F32)
    ln = ln + swap_cores(ln)
    mine = (mine + received).astype(BF16).reshape(peers, 16, width)
    ln = jnp.broadcast_to(jnp.pad(ln, ((0, 8), (0, 0))).astype(BF16)[None], (peers, 16, 128))
    payload = after(jnp.concatenate([d_second, mine, ln], axis=2), back_first)
    moved = exchange(payload)
    total = jnp.sum(moved[:, :, width:].astype(F32), axis=0) * norm
    weights = total[:, :width].astype(BF16)
    full = exchange(jnp.broadcast_to(weights[None], (peers, 16, width)))
    result = jnp.concatenate([back_first, moved[:, :, :width]], axis=1)
    ours = full.reshape(2, width, width)
    theirs = swap_cores(ours)
    low = jnp.where(core == 0, ours, theirs).astype(F32)
    high = jnp.where(core == 0, theirs, ours).astype(F32)
    ln_total = total[:8, width:].reshape(2, width)
    return (
        result.reshape(rows, cols, width),
        jnp.concatenate([low[0], low[1], high[0]], axis=1),
        high[1],
        ln_total[0],
        ln_total[1],
    )


def solution(mesh):
    cores = mesh.devices.reshape(mesh.shape["gx"], mesh.shape["gy"] // 2, 2)
    inner = Mesh(cores, ("gx", "gh", "core"))
    block = P("gx", ("gh", "core"), None)
    return jax.shard_map(
        body,
        mesh=inner,
        in_specs=(block, block, P(), P(), P(), P(), P()),
        out_specs=(block, P(), P(), P(), P()),
        check_vma=False,
    )
```

time: 286 us -> 204 us (0.71); the launches traced: 282 us -> 203 us
  Pallas kernels: 93.2 us -> 48.4 us
  local copies, waits for them, and re-layouts: 24.9 us -> 6.05 us
  starting transfers between devices: 49.2 us -> 35.5 us
  waiting for transfers between devices: 50.5 us -> 37.6 us
  blocking collectives: 50.9 us -> 60.6 us
    pallas_call x3 -> x2, Pallas kernels: 93.2 us -> 48.4 us  [window_pass(): pl.pallas_call(kernel, grid=(windows // STEP,), in_specs=[pl.BlockSpec(me...]
    all_to_all x5 -> x3, starting transfers between devices: 42.5 us -> 28.5 us  [exchange(): lax.all_to_all(array, ('gx', 'gh'), split_axis=0, concat_axis=0, tiled=True)]
    unnamed x30 -> x8, local copies, waits for them, and re-layouts: 12.1 us -> 0.02 us
    all_to_all x5 -> x3, waiting for transfers between devices: 47.7 us -> 36.7 us  [exchange(): lax.all_to_all(array, ('gx', 'gh'), split_axis=0, concat_axis=0, tiled=True)]
    all_to_all x2, blocking collectives: 50.9 us -> 60.6 us  [exchange(): lax.all_to_all(array, ('gx', 'gh'), split_axis=0, concat_axis=0, tiled=True)]
    slice x7 -> x3, local copies, waits for them, and re-layouts: 11.5 us -> 2.98 us  [the longest x1 2.85 us: body(): first = jnp.concatenate([latent[:, :half], cotangent[:, :half]], axis=1)]
    concatenate x2 -> x5, other arithmetic: 3.44 us -> 9.2 us  [the longest x1 2.71 us: body(): result = jnp.concatenate([back_first, moved[:, :, :width]], axis=1)]
    ppermute x2 -> x3, starting transfers between devices: 6.71 us -> 7.01 us  [swap_cores(): return lax.ppermute(array, 'core', [(0, 1), (1, 0)])]
  transfers between devices with their start and end apart: 7 -> 6, of which waited for: 4 -> 4; matrix products, arithmetic and copies ran while one was open for 3% -> 5% of each run, Pallas kernels for 24% -> 12%
where the time goes in v2:
time: 204 us; the launch traced here: 203 us
  blocking collectives  60.6 us (30%)
  Pallas kernels  48.4 us (24%)
  waiting for transfers between devices  37.6 us (18%)
  starting transfers between devices  35.5 us (17%)
  other arithmetic  13 us (6%)
  local copies, waits for them, and re-layouts  6.05 us (3%)
    all_to_all x2, blocking collectives, exchange(): lax.all_to_all(array, ('gx', 'gh'), split_axis=0, concat_axis=0, tiled=True)  60.6 us
    pallas_call x2, Pallas kernels, window_pass(): pl.pallas_call(kernel, grid=(windows // STEP,), in_specs=[pl.BlockSpec(me...  48.4 us
    all_to_all x3, waiting for transfers between devices, exchange(): lax.all_to_all(array, ('gx', 'gh'), split_axis=0, concat_axis=0, tiled=True)  36.7 us
    all_to_all x3, starting transfers between devices, exchange(): lax.all_to_all(array, ('gx', 'gh'), split_axis=0, concat_axis=0, tiled=True)  28.5 us
    ppermute x3, starting transfers between devices, swap_cores(): return lax.ppermute(array, 'core', [(0, 1), (1, 0)])  7.01 us
  transfers between devices with their start and end apart: 6, of which 4 were waited for; matrix products, arithmetic and copies ran while one was open for 5% of the time, Pallas kernels for 12%

profile of v2, /device:TPU:1, one launch (start us, length us, event | category | flops | bytes accessed | tf_op | source)
XLA Modules:
  0.0 203.2 jit_solution(2680782195311854063)
XLA Ops:
  0.6 0.0 copy-start
  0.6 2.8 %fusion.2 = (bf16[64,16,512]{2,1,0:T(8,128)(2,1)S(1)}, bf16[64,16,512]{2,1,0:T(8,128)(2,1)S(1)}, bf16[64,16,512]{2,1,0:T(8,128)(2,1)S(1)}, bf16[64,16,512]{2,1,0:T(8,128)(2,1)S(1)}) fusion(bf16[64,32,512]{2,1,0:T(8,128)(2,1)} %bitcast.38, bf16[64,32,512]{2,1,0:T(8,128)(2,1)} %bitcast.39), kind=kLoop, calls=%fused_computation.34 | loop fusion | bytes 8388608 | tf_op jit(solution)/shard_map/slice | solution.py:272
  3.5 1.5 pad_maximum_fusion.2
  5.0 12.2 %all-to-all-start = ((bf16[64,32,512]{2,1,0:T(8,128)(2,1)}), bf16[64,32,512]{2,1,0:T(8,128)(2,1)}, u32[]{:S(2)}, u32[]{:S(2)}) async-start(bf16[64,32,512]{2,1,0:T(8,128)(2,1)} %pad_maximum_fusion.2), calls=%async_computation | async-start | bytes 4194304 | tf_op jit(solution)/shard_map/all_to_all | solution.py:245
  17.3 0.1 add_add_fusion
  17.4 0.1 add.66
  17.4 0.0 copy-done
  17.4 1.3 convolution_bitcast_fusion
  18.8 0.2 reshape.176
  19.0 0.3 copy.14
  19.3 0.3 reshape.177.refs_6_
  19.7 1.5 pad_maximum_fusion.3
  21.2 0.0 copy-start.1
  21.2 0.0 copy-start.2
  21.2 0.0 copy-start.3
  21.2 23.1 %all-to-all-done.refs_1_ = bf16[64,32,512]{2,1,0:T(8,128)(2,1)} async-done(((bf16[64,32,512]{2,1,0:T(8,128)(2,1)}), bf16[64,32,512]{2,1,0:T(8,128)(2,1)}, u32[]{:S(2)}, u32[]{:S(2)}) %all-to-all-start) | async-done | bytes 2097184 | tf_op jit(solution)/shard_map/all_to_all | solution.py:245
  44.3 8.5 %all-to-all-start.2 = ((bf16[64,32,512]{2,1,0:T(8,128)(2,1)}), bf16[64,32,512]{2,1,0:T(8,128)(2,1)}, u32[]{:S(2)}, u32[]{:S(2)}) async-start(bf16[64,32,512]{2,1,0:T(8,128)(2,1)} %pad_maximum_fusion.3), calls=%async_computation.2 | async-start | bytes 4194304 | tf_op jit(solution)/shard_map/all_to_all | solution.py:245
  52.8 0.0 copy-done.1
  52.8 0.0 copy-done.2
  52.8 0.0 copy-done.3
  52.9 23.8 %window_first.1 = (bf16[64,16,512]{2,1,0:T(8,128)(2,1)}, f32[4,512,512]{2,1,0:T(8,128)}, f32[2,8,512]{2,1,0:T(8,128)S(1)}) custom-call(s32[1]{0:T(128)} %bitcast.refs_0_, bf16[64,32,512]{2,1,0:T(8,128)(2,1)} %all-to-all-done.refs_1_, f32[1,512]{1,0:T(1,128)S(1)} %bitcast.29, f32[1,512]{1,0:T(1,128)S(1)} %bitcast.31, bf16[512,1536]{1,0:T(8,128)(2,1)} %refs_4_.3, ...), custom_call_target="tpu_custom_call" | custom-call | flops 24999999488 | bytes 20971520 | tf_op jit(solution)/shard_map/window_first/pallas_call | solution.py:206
  76.6 1.7 all-to-all-done.2.refs_1_
  78.3 24.7 %window_last.1 = (bf16[64,16,512]{2,1,0:T(8,128)(2,1)S(1)}, f32[2,512,512]{2,1,0:T(8,128)}, bf16[2,512,512]{2,1,0:T(8,128)(2,1)}, f32[2,8,512]{2,1,0:T(8,128)S(1)}) custom-call(s32[1]{0:T(128)} %bitcast.refs_0_, bf16[64,32,512]{2,1,0:T(8,128)(2,1)} %all-to-all-done.2.refs_1_, f32[1,512]{1,0:T(1,128)S(1)} %bitcast.30, f32[1,512]{1,0:T(1,128)S(1)} %bitcast.32, ...), custom_call_target="tpu_custom_call" | custom-call | flops 24999999488 | bytes 20971520 | tf_op jit(solution)/shard_map/window_last/pallas_call | solution.py:206
  103.0 3.8 %collective-permute-start = (bf16[2,512,512]{2,1,0:T(8,128)(2,1)}, bf16[2,512,512]{2,1,0:T(8,128)(2,1)S(1)}, u32[]{:S(2)}, u32[]{:S(2)}) collective-permute-start(bf16[2,512,512]{2,1,0:T(8,128)(2,1)} %get-tuple-element.20), channel_id=1, source_target_pairs={{0,1},{1,0},{2,3},{3,2},{4,5},{5,4},{6,7},{7,6},{8,9},{9,8},{10,11... | collective-permute-start | bytes 3145736 | tf_op jit(solution)/shard_map/ppermute | solution.py:249
  106.8 7.7 %all-to-all-start.1 = ((bf16[64,16,512]{2,1,0:T(8,128)(2,1)}), bf16[64,16,512]{2,1,0:T(8,128)(2,1)}, u32[]{:S(2)}, u32[]{:S(2)}) async-start(bf16[64,16,512]{2,1,0:T(8,128)(2,1)} %get-tuple-element.14), calls=%async_computation.1 | async-start | bytes 2097152 | tf_op jit(solution)/shard_map/all_to_all | solution.py:245
  114.5 0.4 collective-permute-start.1
  114.9 0.9 collective-permute-done.1
  115.8 0.0 collective-permute-done
  115.8 1.9 add_convert_fusion
  117.8 1.6 pad_maximum_fusion.1
  119.4 11.9 %all-to-all-done.1 = bf16[64,16,512]{2,1,0:T(8,128)(2,1)} async-done(((bf16[64,16,512]{2,1,0:T(8,128)(2,1)}), bf16[64,16,512]{2,1,0:T(8,128)(2,1)}, u32[]{:S(2)}, u32[]{:S(2)}) %all-to-all-start.1) | async-done | bytes 1048608 | tf_op jit(solution)/shard_map/all_to_all | solution.py:245
  131.3 36.6 %all_to_all.25 = bf16[64,16,1152]{2,1,0:T(8,128)(2,1)S(1)} all-to-all(bf16[64,16,1152]{2,1,0:T(8,128)(2,1)} %pad_maximum_fusion.1), channel_id=1, replica_groups=mesh['gx'=8,'gh'=8,'core'=2] {'gx','gh'}, dimensions={0} | all-to-all | bytes 4718592 | tf_op jit(solution)/shard_map/all_to_all | solution.py:245
  167.9 0.2 convert_reduce_fusion
  168.1 0.1 broadcast_in_dim.10
  168.2 24.0 %all_to_all.26 = bf16[64,16,512]{2,1,0:T(8,128)(2,1)S(1)} all-to-all(bf16[64,16,512]{2,1,0:T(8,128)(2,1)S(1)} %broadcast_in_dim.10), channel_id=1, replica_groups=mesh['gx'=8,'gh'=8,'core'=2] {'gx','gh'}, dimensions={0} | all-to-all | bytes 2097152 | tf_op jit(solution)/shard_map/all_to_all | solution.py:245
  192.3 2.8 %collective-permute-start.2 = (bf16[2,512,512]{2,1,0:T(8,128)(2,1)S(1)}, bf16[2,512,512]{2,1,0:T(8,128)(2,1)}, u32[]{:S(2)}, u32[]{:S(2)}) collective-permute-start(bf16[2,512,512]{2,1,0:T(8,128)(2,1)S(1)} %bitcast.33), channel_id=1, source_target_pairs={{0,1},{1,0},{2,3},{3,2},{4,5},{5,4},{6,7},{7,6},{8,9},{9,8},{10,11... | collective-permute-start | bytes 3145736 | tf_op jit(solution)/shard_map/ppermute | solution.py:249
  195.1 0.1 slice.62
  195.2 2.7 %pad_maximum_fusion.4 = bf16[64,32,512]{2,1,0:T(8,128)(2,1)} fusion(bf16[64,16,512]{2,1,0:T(8,128)(2,1)S(1)} %slice.62, bf16[64,16,512]{2,1,0:T(8,128)(2,1)} %all-to-all-done.1), kind=kLoop, calls=%fused_computation.7 | loop fusion | flops 4194304 | bytes 4194304 | tf_op jit(solution)/shard_map/concatenate | solution.py:290
  198.0 0.6 slice_bitcast_fusion.4
  198.5 0.0 collective-permute-done.2
  198.5 1.5 select_convert_fusion.1
  200.1 1.1 slice_bitcast_fusion
  201.2 0.2 slice_bitcast_fusion.3
  201.4 1.9 pad_maximum_fusion
  (11 shorter events, 0.1 us)
Async XLA Ops:
  0.6 16.8 %copy-start = (f32[16,225]{1,0:T(8,128)S(1)}, f32[16,225]{1,0:T(8,128)}, u32[]{:S(2)}) copy-start(f32[16,225]{1,0:T(8,128)} %param.13) | copy-start | bytes 43204
  5.0 39.3 %all-to-all-start = ((bf16[64,32,512]{2,1,0:T(8,128)(2,1)}), bf16[64,32,512]{2,1,0:T(8,128)(2,1)}, u32[]{:S(2)}, u32[]{:S(2)}) async-start(bf16[64,32,512]{2,1,0:T(8,128)(2,1)} %pad_maximum_fusion.2), calls=%async_computation | async-start | bytes 4194304 | tf_op jit(solution)/shard_map/all_to_all | solution.py:245
  21.2 31.6 %copy-start.1 = (bf16[512,512]{1,0:T(8,128)(2,1)S(1)}, bf16[512,512]{1,0:T(8,128)(2,1)}, u32[]{:S(2)}) copy-start(bf16[512,512]{1,0:T(8,128)(2,1)} %refs_5_.3) | copy-start | bytes 1572868
  21.2 31.6 %copy-start.2 = (f32[512]{0:T(512)S(1)}, f32[512]{0:T(512)}, u32[]{:S(2)}) copy-start(f32[512]{0:T(512)} %param.9) | copy-start | bytes 6148
  21.2 31.6 %copy-start.3 = (f32[512]{0:T(512)S(1)}, f32[512]{0:T(512)}, u32[]{:S(2)}) copy-start(f32[512]{0:T(512)} %param.10) | copy-start | bytes 6148
  44.3 34.0 %all-to-all-start.2 = ((bf16[64,32,512]{2,1,0:T(8,128)(2,1)}), bf16[64,32,512]{2,1,0:T(8,128)(2,1)}, u32[]{:S(2)}, u32[]{:S(2)}) async-start(bf16[64,32,512]{2,1,0:T(8,128)(2,1)} %pad_maximum_fusion.3), calls=%async_computation.2 | async-start | bytes 4194304 | tf_op jit(solution)/shard_map/all_to_all | solution.py:245
  103.0 12.9 %collective-permute-start = (bf16[2,512,512]{2,1,0:T(8,128)(2,1)}, bf16[2,512,512]{2,1,0:T(8,128)(2,1)S(1)}, u32[]{:S(2)}, u32[]{:S(2)}) collective-permute-start(bf16[2,512,512]{2,1,0:T(8,128)(2,1)} %get-tuple-element.20), channel_id=1, source_target_pairs={{0,1},{1,0},{2,3},{3,2},{4,5},{5,4},{6,7},{7,6},{8,9},{9,8},{10,11... | collective-permute-start | bytes 3145736 | tf_op jit(solution)/shard_map/ppermute | solution.py:249
  106.8 24.6 %all-to-all-start.1 = ((bf16[64,16,512]{2,1,0:T(8,128)(2,1)}), bf16[64,16,512]{2,1,0:T(8,128)(2,1)}, u32[]{:S(2)}, u32[]{:S(2)}) async-start(bf16[64,16,512]{2,1,0:T(8,128)(2,1)} %get-tuple-element.14), calls=%async_computation.1 | async-start | bytes 2097152 | tf_op jit(solution)/shard_map/all_to_all | solution.py:245
  114.5 1.2 collective-permute-start.1
  192.3 6.3 %collective-permute-start.2 = (bf16[2,512,512]{2,1,0:T(8,128)(2,1)S(1)}, bf16[2,512,512]{2,1,0:T(8,128)(2,1)}, u32[]{:S(2)}, u32[]{:S(2)}) collective-permute-start(bf16[2,512,512]{2,1,0:T(8,128)(2,1)S(1)} %bitcast.33), channel_id=1, source_target_pairs={{0,1},{1,0},{2,3},{3,2},{4,5},{5,4},{6,7},{7,6},{8,9},{9,8},{10,11... | collective-permute-start | bytes 3145736 | tf_op jit(solution)/shard_map/ppermute | solution.py:249

commit v3 on v2

v3 whole, which is shorter than its diff:
```python
import math

import jax
import jax.numpy as jnp
from jax import lax
from jax.experimental import pallas as pl
from jax.experimental.pallas import tpu as pltpu
from jax.sharding import Mesh, PartitionSpec as P

F32 = jnp.float32
BF16 = jnp.bfloat16
HEADS = 16
CELLS = 64
PARTS = 2
STEP = 8
ROWS = STEP * CELLS
GROUPS = 4
FACTOR = 1.0 / math.sqrt(32.0)
NATURAL = (0, 1, 2, 3)
SWAPPED = (0, 2, 1, 3)
SKEW = 1
CHUNKS = 4
CHUNK = CELLS // CHUNKS
VMEM_MIB = 60
MIB = 1 << 20


def dot(left, right):
    return jnp.dot(left, right, preferred_element_type=F32)


def dot_cols(left, right):
    return lax.dot_general(left, right, (((1,), (1,)), ((), ())), preferred_element_type=F32)


def dot_rows(left, right):
    return lax.dot_general(left, right, (((0,), (0,)), ((), ())), preferred_element_type=F32)


def spread(block, mask_ref, order):
    return jnp.concatenate([block * mask_ref[h] for h in order], axis=0)


def turn(block):
    tall = jnp.concatenate([block[:, :128], block[:, 128:]], axis=0)
    tall = tall.T
    return jnp.concatenate([tall[:64], tall[64:]], axis=1)


def window_rows(slab, first, windows):
    return jnp.concatenate(
        [
            jnp.concatenate(
                [slab[k, pl.ds(first + j, CELLS, stride=windows), :] for j in range(STEP)], axis=0
            )
            for k in range(4)
        ],
        axis=1,
    )


def standardise(values):
    centred = values - jnp.mean(values, -1, keepdims=True)
    variance = jnp.mean(centred * centred, -1, keepdims=True)
    inverse = lax.rsqrt(variance + 1e-05)
    return centred * inverse, inverse


def unit(j, g, qkv, d_att, d_qkv, att, bias_ref, mask_ref):
    rows = pl.ds(j * CELLS, CELLS)
    lane = g * 128
    q4 = qkv[rows, lane : lane + 128]
    k4 = qkv[rows, 512 + lane : 512 + lane + 128]
    v4 = qkv[rows, 1024 + lane : 1024 + lane + 128]
    q_wide = spread(q4, mask_ref, NATURAL)
    d_att_wide = spread(d_att[rows, lane : lane + 128], mask_ref, NATURAL)
    scores = dot_cols(k4, q_wide) * FACTOR + bias_ref[g]
    d_probs = dot_cols(v4, d_att_wide)
    yield
    probs = jnp.exp(scores - jnp.max(scores, 0, keepdims=True))
    probs = probs * (1.0 / jnp.sum(probs, 0, keepdims=True))
    probs_b = probs.astype(BF16)
    yield
    d_scores = probs * (d_probs - jnp.sum(probs * d_probs, 0, keepdims=True))
    ds_b = d_scores.astype(BF16)
    yield
    turned = turn(probs_b)
    ds_turned = turn(ds_b)
    yield
    attended = dot(turned, spread(v4, mask_ref, SWAPPED))
    d_query = dot(ds_turned, spread(k4, mask_ref, SWAPPED)) * FACTOR
    d_keys = dot(ds_b, q_wide) * FACTOR
    d_vals = dot(probs_b, d_att_wide)
    att[rows, lane : lane + 128] = attended.astype(BF16)
    d_qkv[rows, lane : lane + 128] = d_query.astype(BF16)
    d_qkv[rows, 512 + lane : 512 + lane + 128] = d_keys.astype(BF16)
    d_qkv[rows, 1024 + lane : 1024 + lane + 128] = d_vals.astype(BF16)


def interleave(units, skew):
    running = []
    time = 0
    units = list(units)
    while units or running:
        if units and time % skew == 0:
            running.append(units.pop(0))
        alive = [u for u in reversed(running) if next(u, True) is not True]
        running = alive[::-1]
        time += 1


def copies_in(pairs, sems):
    copies = [
        pltpu.make_async_copy(source, target, sems.at[i])
        for i, (source, target) in enumerate(pairs)
    ]
    for copy in copies:
        copy.start()
    return copies


def chunk_copy(source, target, sems, c):
    part = pl.ds(c * CHUNK, CHUNK)
    return pltpu.make_async_copy(source.at[part], target.at[part], sems.at[c])


def window_kernel(*refs, last):
    core_ref, x_any, gain_ref, shift_ref, wqkv_any, wout_any, bias_any, mask_ref = refs[:8]
    refs = refs[8:]
    if last:
        gw_any, ln_in, out_any, other_any, ln_out = refs[:5]
        other, gw_before, ln_ref = refs[-3:]
        refs = refs[5:-3]
    else:
        out_any, gw_any, ln_ref = refs[:3]
        refs = refs[3:]
    x_ref, wqkv_ref, wout_ref, bias_ref, gw_ref, out_ref = refs[:6]
    lat_slab, cot_slab, qkv, d_att, d_qkv, att, x_sems, sems, out_sems = refs[6:]
    windows = x_ref.shape[1] // 2

    for c in range(CHUNKS):
        chunk_copy(x_any, x_ref, x_sems, c).start()
    pairs = [(wout_any, wout_ref), (wqkv_any, wqkv_ref), (bias_any, bias_ref)]
    if last:
        ln_ref[...] = ln_in[...]
    else:
        ln_ref[...] = jnp.zeros_like(ln_ref)
    loads = copies_in(pairs, sems)
    gw_ref[...] = jnp.zeros_like(gw_ref)

    def fill(c, carry):
        chunk_copy(x_any, x_ref, x_sems, c).wait()
        for i in range(CHUNK):
            n = c * CHUNK + i
            rows = pl.ds(pl.multiple_of(n * windows, windows), windows)
            for k in range(4):
                lanes = slice(k * 128, k * 128 + 128)
                lat_slab[k, rows, :] = x_ref[n, :windows, lanes].astype(F32)
                cot_slab[k, rows, :] = x_ref[n, windows:, lanes].astype(F32)
        return carry

    lax.fori_loop(0, CHUNKS, fill, 0)
    for load in loads:
        load.wait()
    if last:
        before = pltpu.make_async_copy(gw_any, gw_before, sems.at[3])
        before.start()

    def step(t, carry):
        cot = window_rows(cot_slab, t * STEP, windows)
        cot_b = cot.astype(BF16)
        d_att[...] = dot_cols(cot_b, wout_ref[...]).astype(BF16)
        xhat, inverse = standardise(window_rows(lat_slab, t * STEP, windows))
        normed = (xhat * gain_ref[...] + shift_ref[...]).astype(BF16)
        qkv[...] = dot(normed, wqkv_ref[...]).astype(BF16)
        interleave(
            (
                unit(j, g, qkv, d_att, d_qkv, att, bias_ref, mask_ref)
                for j in range(STEP)
                for g in range(GROUPS)
            ),
            SKEW,
        )
        for k in range(3):
            gw_ref[k] += dot_rows(normed, d_qkv[:, k * 512 : k * 512 + 512])
        gw_ref[3] += dot_rows(att[...], cot_b)
        d_normed = dot_cols(d_qkv[...], wqkv_ref[...])
        weighted = xhat * d_normed
        ln_ref[0] += jnp.sum(weighted.reshape(ROWS // 8, 8, 512), 0)
        ln_ref[1] += jnp.sum(d_normed.reshape(ROWS // 8, 8, 512), 0)
        d_hat = d_normed * gain_ref[...]
        value = cot + inverse * (
            d_hat
            - jnp.mean(d_hat, -1, keepdims=True)
            - xhat * jnp.mean(d_hat * xhat, -1, keepdims=True)
        )
        for j in range(STEP):
            for k in range(4):
                lat_slab[k, pl.ds(t * STEP + j, CELLS, stride=windows), :] = value[
                    j * CELLS : j * CELLS + CELLS, k * 128 : k * 128 + 128
                ]
        return carry

    lax.fori_loop(0, windows // STEP, step, 0)

    stores = []
    if last:
        for part in range(2):
            sums = jnp.sum(ln_ref[part], 0, keepdims=True)
            for k in range(4):
                row = part * 4 + k
                ln_out[row : row + 1, :] = sums[:, k * 128 : k * 128 + 128]
        before.wait()
        core = core_ref[0]
        for k in range(2):
            block = 2 * (1 - core) + k
            other[:, k * 512 : k * 512 + 512] = (gw_ref[block] + gw_before[block]).astype(BF16)
        stores.append(pltpu.make_async_copy(other, other_any, sems.at[0]))
    else:
        stores.append(pltpu.make_async_copy(gw_ref, gw_any, sems.at[0]))
    stores[0].start()

    def empty(c, carry):
        for i in range(CHUNK):
            n = c * CHUNK + i
            rows = pl.ds(pl.multiple_of(n * windows, windows), windows)
            for k in range(4):
                cells = lat_slab[k, rows, :].astype(BF16)
                lane = k * 128
                if last:
                    out_ref[n, :, lane : lane + 128] = cells[:8]
                    out_ref[n, :, 512 + lane : 512 + lane + 128] = cells[8:]
                else:
                    out_ref[n, :, lane : lane + 128] = cells
            if last:
                mine = pl.ds(pl.multiple_of(n * 8, 8), 8)
                for k in range(2):
                    block = 2 * core + k
                    out_ref[n, :, 1024 + k * 512 : 1536 + k * 512] = (
                        gw_ref[block, mine, :] + gw_before[block, mine, :]
                    ).astype(BF16)
        chunk_copy(out_ref, out_any, out_sems, c).start()
        return carry

    lax.fori_loop(0, CHUNKS, empty, 0)
    for c in range(CHUNKS):
        stores.append(chunk_copy(out_ref, out_any, out_sems, c))
    for store in stores:
        store.wait()


def window_pass(core, x, gain, shift, w_qkv, w_out, bias, mask, sums):
    last = sums is not None
    windows = x.shape[1] // 2
    cells = windows * CELLS
    shape = jax.ShapeDtypeStruct
    everywhere = pl.BlockSpec(memory_space=pl.ANY)
    vmem = pl.BlockSpec(memory_space=pltpu.VMEM)
    grads = shape((4, 512, 512), F32)
    ln = shape((2, 8, 512), F32)
    if last:
        outs = [shape((CELLS, 8, 2048), BF16), shape((512, 1024), BF16), shape((8, 128), F32)]
    else:
        outs = [shape((CELLS, windows, 512), BF16), grads, ln]

    def kernel(*refs):
        window_kernel(*refs, last=last)

    return pl.pallas_call(
        kernel,
        in_specs=[
            pl.BlockSpec(memory_space=pltpu.SMEM),
            everywhere, vmem, vmem, everywhere, everywhere, everywhere, vmem,
        ]
        + ([everywhere, vmem] if last else []),
        out_specs=[everywhere, everywhere, vmem],
        out_shape=outs,
        scratch_shapes=[
            pltpu.VMEM(x.shape, BF16),
            pltpu.VMEM(w_qkv.shape, BF16),
            pltpu.VMEM(w_out.shape, BF16),
            pltpu.VMEM(bias.shape, F32),
            pltpu.VMEM(grads.shape, F32),
            pltpu.VMEM(outs[0].shape, BF16),
            pltpu.VMEM((4, cells, 128), F32),
            pltpu.VMEM((4, cells, 128), F32),
            pltpu.VMEM((ROWS, 1536), BF16),
            pltpu.VMEM((ROWS, 512), BF16),
            pltpu.VMEM((ROWS, 1536), BF16),
            pltpu.VMEM((ROWS, 512), BF16),
            pltpu.SemaphoreType.DMA((CHUNKS,)),
            pltpu.SemaphoreType.DMA((4,)),
            pltpu.SemaphoreType.DMA((CHUNKS,)),
        ]
        + (
            [
                pltpu.VMEM((512, 1024), BF16),
                pltpu.VMEM(grads.shape, F32),
                pltpu.VMEM(ln.shape, F32),
            ]
            if last
            else []
        ),
        compiler_params=pltpu.CompilerParams(vmem_limit_bytes=VMEM_MIB * MIB),
        cost_estimate=pl.CostEstimate(
            flops=20 * 10**9, bytes_accessed=12 * MIB, transcendentals=10**6
        ),
        name="window_last" if last else "window_first",
    )(core, x, gain, shift, w_qkv, w_out, bias, mask, *(sums or ()))


def pack(latent, cotangent, part, half):
    peers, _, width = latent.shape
    pieces = 4
    size = peers // pieces

    def kernel(latent_any, cotangent_any, out_any, held, in_sems, out_sems):
        def load(c, k):
            block = pl.ds(c * size, size)
            source = (latent_any, cotangent_any)[k]
            return pltpu.make_async_copy(
                source.at[block, pl.ds(part * half, half)],
                held.at[block, pl.ds(k * half, half)],
                in_sems.at[2 * c + k],
            )

        def store(c):
            block = pl.ds(c * size, size)
            return pltpu.make_async_copy(held.at[block], out_any.at[block], out_sems.at[c])

        for c in range(pieces):
            load(c, 0).start()
            load(c, 1).start()
        for c in range(pieces):
            load(c, 0).wait()
            load(c, 1).wait()
            store(c).start()
        for c in range(pieces):
            store(c).wait()

    everywhere = pl.BlockSpec(memory_space=pl.ANY)
    return pl.pallas_call(
        kernel,
        in_specs=[everywhere, everywhere],
        out_specs=everywhere,
        out_shape=jax.ShapeDtypeStruct((peers, 2 * half, width), BF16),
        scratch_shapes=[
            pltpu.VMEM((peers, 2 * half, width), BF16),
            pltpu.SemaphoreType.DMA((2 * pieces,)),
            pltpu.SemaphoreType.DMA((pieces,)),
        ],
        compiler_params=pltpu.CompilerParams(vmem_limit_bytes=VMEM_MIB * MIB),
        cost_estimate=pl.CostEstimate(flops=0, bytes_accessed=4 * MIB, transcendentals=0),
        name="pack_part",
    )(latent, cotangent)


def join_kernel(core_ref, ours_ref, theirs_ref, gq_ref, go_ref):
    own = core_ref[0] == 0
    ours = ours_ref[:, :1024].astype(F32)
    theirs = theirs_ref[:, :1024].astype(F32)
    gq_ref[:, :1024] = jnp.where(own, ours, theirs)
    high = jnp.where(own, theirs, ours)
    gq_ref[:, 1024:] = high[:, :512]
    go_ref[...] = high[:, 512:]


def join(core, ours, theirs):
    def block(width):
        return pl.BlockSpec((128, width), lambda i: (i, 0))

    return pl.pallas_call(
        join_kernel,
        grid=(4,),
        in_specs=[pl.BlockSpec(memory_space=pltpu.SMEM), block(1152), block(1152)],
        out_specs=[block(1536), block(512)],
        out_shape=[
            jax.ShapeDtypeStruct((512, 1536), F32),
            jax.ShapeDtypeStruct((512, 512), F32),
        ],
        compiler_params=pltpu.CompilerParams(vmem_limit_bytes=8 * MIB),
        name="join_halves",
    )(core, ours, theirs)


def bias_tables(rel_bias):
    position = jnp.arange(CELLS, dtype=jnp.int32)
    prow = position // 8
    pcol = position % 8
    offset = (prow[None, :] - prow[:, None] + 7) * 15 + (pcol[None, :] - pcol[:, None] + 7)
    onehot = (offset.reshape(1, -1) == jnp.arange(225, dtype=jnp.int32)[:, None]).astype(F32)
    full = jnp.dot(rel_bias, onehot, precision=lax.Precision.HIGHEST)
    full = full.reshape(GROUPS, HEADS // GROUPS, CELLS, CELLS).transpose(0, 2, 1, 3)
    return full.reshape(GROUPS, CELLS, 256)


def after(value, *others):
    return lax.optimization_barrier((value,) + others)[0]


def exchange(array):
    return lax.all_to_all(array, ("gx", "gh"), split_axis=0, concat_axis=0, tiled=True)


def swap_cores(array):
    return lax.ppermute(array, "core", [(0, 1), (1, 0)])


def body(latent, cotangent, gain, shift, w_qkv, w_out, rel_bias):
    rows, cols, width = latent.shape
    peers = lax.axis_size("gx") * lax.axis_size("gh")
    windows = rows * cols // peers
    half = windows // PARTS
    norm = 1.0 / math.sqrt(rows * cols * peers * lax.axis_size("core"))
    core = lax.axis_index("core")
    gain = gain.reshape(1, width)
    shift = shift.reshape(1, width)
    lane = jnp.arange(128, dtype=jnp.int32) // 32
    mask = jnp.broadcast_to(
        (lane[None, None, :] == jnp.arange(4, dtype=jnp.int32)[:, None, None]).astype(BF16),
        (4, CELLS, 128),
    )
    bias = bias_tables(rel_bias)
    consts = (gain, shift, w_qkv, w_out, bias, mask)
    core_id = core.astype(jnp.int32).reshape(1)

    latent = latent.reshape(peers, windows, width)
    cotangent = cotangent.reshape(peers, windows, width)
    x_first = exchange(pack(latent, cotangent, 0, half))
    x_second = exchange(after(pack(latent, cotangent, 1, half), x_first))
    d_first, gw, ln = window_pass(core_id, x_first, *consts, None)
    back_first = exchange(d_first)
    payload, other, ln = window_pass(core_id, x_second, *consts, (gw, ln))

    other, ln = lax.optimization_barrier((other, ln, back_first))[:2]
    received = swap_cores(other).reshape(peers, 8, 1024)
    ln = ln + swap_cores(ln)
    mine = payload[:, :, 1024:].astype(F32) + received.astype(F32)
    moved = exchange(payload.at[:, :, 1024:].set(mine.astype(BF16)))
    total = jnp.sum(moved[:, :, 1024:].astype(F32), axis=0) * norm
    share = jnp.concatenate([total, ln], axis=1).astype(BF16)
    full = exchange(jnp.broadcast_to(share[None], (peers, 8, 1152)))
    result = jnp.concatenate(
        [back_first, moved[:, :, :width], moved[:, :, width : 2 * width]], axis=1
    )
    full, result = lax.optimization_barrier((full, result))
    ours = full.reshape(width, 1152)
    grad_qkv, grad_out = join(core_id, ours, swap_cores(ours))
    ln_total = (jnp.sum(full[:, :, 1024:].astype(F32), axis=0) * norm).reshape(2, width)
    return (result.reshape(rows, cols, width), grad_qkv, grad_out, ln_total[0], ln_total[1])


def solution(mesh):
    cores = mesh.devices.reshape(mesh.shape["gx"], mesh.shape["gy"] // 2, 2)
    inner = Mesh(cores, ("gx", "gh", "core"))
    block = P("gx", ("gh", "core"), None)
    return jax.shard_map(
        body,
        mesh=inner,
        in_specs=(block, block, P(), P(), P(), P(), P()),
        out_specs=(block, P(), P(), P(), P()),
        check_vma=False,
    )
```

time: 204 us -> 187 us (0.917)
  blocking collectives: 60.6 us -> 0 us
  waiting for transfers between devices: 37.6 us -> 71.8 us
  starting transfers between devices: 35.5 us -> 54.4 us
  other arithmetic: 13 us -> 4.53 us
    all_to_all x2 -> x0, blocking collectives: 60.6 us -> none  [exchange(): lax.all_to_all(array, ('gx', 'gh'), split_axis=0, concat_axis=0, tiled=True)]
    all_to_all x3 -> x5, waiting for transfers between devices: 36.7 us -> 66.7 us  [exchange(): lax.all_to_all(array, ('gx', 'gh'), split_axis=0, concat_axis=0, tiled=True)]
    all_to_all x3 -> x5, starting transfers between devices: 28.5 us -> 47.1 us  [exchange(): lax.all_to_all(array, ('gx', 'gh'), split_axis=0, concat_axis=0, tiled=True)]
    concatenate x5 -> x2, other arithmetic: 9.2 us -> 1.58 us  [the longest x1 1.57 us: body(): jnp.concatenate([back_first, moved[:, :, :width], moved[:, :, width:2 * w...]
    ppermute x3, waiting for transfers between devices: 0.89 us -> 5.13 us  [swap_cores(): return lax.ppermute(array, 'core', [(0, 1), (1, 0)])]
    convert_element_type x2 -> x0, other arithmetic: 3.44 us -> none  [the longest x1 1.94 us: body(): mine = (mine + received).astype(BF16).reshape(peers, 16, width)]
    slice x3 -> x1, local copies, waits for them, and re-layouts: 2.98 us -> 0.09 us  [body(): moved[:, :, :width]]
    scatter x0 -> x1, other arithmetic: none -> 2.59 us  [body(): moved = exchange(payload.at[:, :, 1024:].set(mine.astype(BF16)))]
  transfers between devices with their start and end apart: 6 -> 8, of which waited for: 4 -> 7; matrix products, arithmetic and copies ran while one was open for 5% -> 3% of each run, Pallas kernels for 12% -> 23%
where the time goes in v3:
time: 187 us; the launch traced here: 186 us
  waiting for transfers between devices  71.8 us (38%)
  starting transfers between devices  54.4 us (29%)
  Pallas kernels  47.9 us (26%)
  local copies, waits for them, and re-layouts  5.25 us (3%)
  other arithmetic  4.53 us (2%)
    all_to_all x5, waiting for transfers between devices, exchange(): lax.all_to_all(array, ('gx', 'gh'), split_axis=0, concat_axis=0, tiled=True)  66.7 us
    all_to_all x5, starting transfers between devices, exchange(): lax.all_to_all(array, ('gx', 'gh'), split_axis=0, concat_axis=0, tiled=True)  47.1 us
    pallas_call x2, Pallas kernels, window_pass(): pl.pallas_call(kernel, in_specs=[pl.BlockSpec(memory_space=pltpu.SMEM), e...  40.5 us
    ppermute x3, starting transfers between devices, swap_cores(): return lax.ppermute(array, 'core', [(0, 1), (1, 0)])  7.29 us
    ppermute x3, waiting for transfers between devices, swap_cores(): return lax.ppermute(array, 'core', [(0, 1), (1, 0)])  5.13 us
    pallas_call x2, Pallas kernels, pack(): pl.pallas_call(kernel, in_specs=[everywhere, everywhere], out_specs=every...  4.9 us
  transfers between devices with their start and end apart: 8, of which 7 were waited for; matrix products, arithmetic and copies ran while one was open for 3% of the time, Pallas kernels for 23%

profile of v3, /device:TPU:1, one launch (start us, length us, event | category | flops | bytes accessed | tf_op | source)
XLA Modules:
  0.0 186.0 jit_solution(3782240134782575192)
XLA Ops:
  0.6 0.0 copy-start
  0.6 2.4 %pack_part.3 = bf16[64,32,512]{2,1,0:T(8,128)(2,1)} custom-call(bf16[64,32,512]{2,1,0:T(8,128)(2,1)} %bitcast.22, bf16[64,32,512]{2,1,0:T(8,128)(2,1)} %bitcast.24), custom_call_target="tpu_custom_call" | custom-call | bytes 4194304 | tf_op jit(solution)/shard_map/pack_part/pallas_call | solution.py:342
  3.1 12.0 %all-to-all-start = ((bf16[64,32,512]{2,1,0:T(8,128)(2,1)}), bf16[64,32,512]{2,1,0:T(8,128)(2,1)S(1)}, u32[]{:S(2)}, u32[]{:S(2)}) async-start(bf16[64,32,512]{2,1,0:T(8,128)(2,1)} %pack_part.3), calls=%async_computation | async-start | bytes 4194304 | tf_op jit(solution)/shard_map/all_to_all | solution.py:402
  15.1 2.4 %pack_part.2 = bf16[64,32,512]{2,1,0:T(8,128)(2,1)} custom-call(bf16[64,32,512]{2,1,0:T(8,128)(2,1)} %bitcast.23, bf16[64,32,512]{2,1,0:T(8,128)(2,1)} %bitcast.25), custom_call_target="tpu_custom_call" | custom-call | bytes 4194304 | tf_op jit(solution)/shard_map/pack_part/pallas_call | solution.py:342
  17.6 0.1 add_add_fusion
  17.6 0.1 add.66
  17.7 0.0 copy-done
  17.7 1.3 convolution_bitcast_fusion
  19.1 0.2 reshape.216
  19.3 0.3 copy.14
  19.6 1.1 reshape.217.refs_6_
  20.7 21.6 %all-to-all-done.refs_1_ = bf16[64,32,512]{2,1,0:T(8,128)(2,1)S(1)} async-done(((bf16[64,32,512]{2,1,0:T(8,128)(2,1)}), bf16[64,32,512]{2,1,0:T(8,128)(2,1)S(1)}, u32[]{:S(2)}, u32[]{:S(2)}) %all-to-all-start) | async-done | bytes 2097184 | tf_op jit(solution)/shard_map/all_to_all | solution.py:402
  42.3 0.0 copy-start.3
  42.3 8.0 %all-to-all-start.1 = ((bf16[64,32,512]{2,1,0:T(8,128)(2,1)}), bf16[64,32,512]{2,1,0:T(8,128)(2,1)}, u32[]{:S(2)}, u32[]{:S(2)}) async-start(bf16[64,32,512]{2,1,0:T(8,128)(2,1)} %pack_part.2), calls=%async_computation.1 | async-start | bytes 4194304 | tf_op jit(solution)/shard_map/all_to_all | solution.py:402
  50.3 0.0 copy-done.3
  50.4 0.6 broadcast_in_dim.6.refs_7_
  51.0 19.8 %window_first.1 = (bf16[64,16,512]{2,1,0:T(8,128)(2,1)}, f32[4,512,512]{2,1,0:T(8,128)}, f32[2,8,512]{2,1,0:T(8,128)}) custom-call(s32[1]{0:T(128)} %bitcast.refs_0_.core_ref, bf16[64,32,512]{2,1,0:T(8,128)(2,1)} %copy-done.3, f32[1,512]{1,0:T(1,128)} %bitcast.28, f32[1,512]{1,0:T(1,128)} %bitcast.30, bf16[512,1536]{1,0:T(8,128)(2,1)} %refs_4_.3, ...), custom_call_target="tpu_custom_call" | custom-call | flops 20000000000 | bytes 12582912 | tf_op jit(solution)/shard_map/window_first/pallas_call | solution.py:269
  70.8 4.9 %all-to-all-done.1.refs_1_ = bf16[64,32,512]{2,1,0:T(8,128)(2,1)} async-done(((bf16[64,32,512]{2,1,0:T(8,128)(2,1)}), bf16[64,32,512]{2,1,0:T(8,128)(2,1)}, u32[]{:S(2)}, u32[]{:S(2)}) %all-to-all-start.1) | async-done | bytes 2097184 | tf_op jit(solution)/shard_map/all_to_all | solution.py:402
  75.7 9.1 %all-to-all-start.2 = ((bf16[64,16,512]{2,1,0:T(8,128)(2,1)}), bf16[64,16,512]{2,1,0:T(8,128)(2,1)S(1)}, u32[]{:S(2)}, u32[]{:S(2)}) async-start(bf16[64,16,512]{2,1,0:T(8,128)(2,1)} %get-tuple-element.36), calls=%async_computation.2 | async-start | bytes 2097152 | tf_op jit(solution)/shard_map/all_to_all | solution.py:402
  84.8 20.7 %window_last.1 = (bf16[64,8,2048]{2,1,0:T(8,128)(2,1)}, bf16[512,1024]{1,0:T(8,128)(2,1)}, f32[8,128]{1,0:T(8,128)}) custom-call(s32[1]{0:T(128)} %bitcast.refs_0_.core_ref, bf16[64,32,512]{2,1,0:T(8,128)(2,1)} %all-to-all-done.1.refs_1_, f32[1,512]{1,0:T(1,128)} %bitcast.29, f32[1,512]{1,0:T(1,128)} %bitcast.31, bf16[512,1536]{1,0:T(8,128)(2,1)} %refs_4_.3, ...), custom_call_target="tpu_custom_call" | custom-call | flops 20000000000 | bytes 12582912 | tf_op jit(solution)/shard_map/window_last/pallas_call | solution.py:269
  105.5 0.0 all-to-all-done.2
  105.6 0.0 copy-start.1
  105.6 3.1 %collective-permute-start = (bf16[512,1024]{1,0:T(8,128)(2,1)}, bf16[512,1024]{1,0:T(8,128)(2,1)S(1)}, u32[]{:S(2)}, u32[]{:S(2)}) collective-permute-start(bf16[512,1024]{1,0:T(8,128)(2,1)} %get-tuple-element.37), channel_id=1, source_target_pairs={{0,1},{1,0},{2,3},{3,2},{4,5},{5,4},{6,7},{7,6},{8,9},{9,8},{10,11... | collective-permute-start | bytes 3145736 | tf_op jit(solution)/shard_map/ppermute | solution.py:406
  108.7 2.5 %collective-permute-done = bf16[512,1024]{1,0:T(8,128)(2,1)S(1)} collective-permute-done((bf16[512,1024]{1,0:T(8,128)(2,1)}, bf16[512,1024]{1,0:T(8,128)(2,1)S(1)}, u32[]{:S(2)}, u32[]{:S(2)}) %collective-permute-start) | collective-permute-done | bytes 1048608 | tf_op jit(solution)/shard_map/ppermute | solution.py:406
  111.2 2.6 %fusion.2 = bf16[64,8,2048]{2,1,0:T(8,128)(2,1)} fusion(bf16[64,8,2048]{2,1,0:T(8,128)(2,1)} %get-tuple-element.33, bf16[512,1024]{1,0:T(8,128)(2,1)S(1)} %collective-permute-done), kind=kLoop, calls=%fused_computation.7 | loop fusion | flops 2097152 | bytes 3145728 | tf_op jit(solution)/shard_map/scatter | solution.py:439
  113.8 0.0 copy-start.4
  113.8 0.0 copy-done.1
  113.8 10.1 %all-to-all-start.3 = ((bf16[64,8,2048]{2,1,0:T(8,128)(2,1)}), bf16[64,8,2048]{2,1,0:T(8,128)(2,1)S(1)}, u32[]{:S(2)}, u32[]{:S(2)}) async-start(bf16[64,8,2048]{2,1,0:T(8,128)(2,1)} %fusion.2), calls=%async_computation.3 | async-start | bytes 4194304 | tf_op jit(solution)/shard_map/all_to_all | solution.py:402
  123.9 0.0 copy-done.4
  123.9 0.7 collective-permute-start.1
  124.6 0.8 collective-permute-done.1
  125.5 26.4 %all-to-all-done.3 = bf16[64,8,2048]{2,1,0:T(8,128)(2,1)S(1)} async-done(((bf16[64,8,2048]{2,1,0:T(8,128)(2,1)}), bf16[64,8,2048]{2,1,0:T(8,128)(2,1)S(1)}, u32[]{:S(2)}, u32[]{:S(2)}) %all-to-all-start.3) | async-done | bytes 2097184 | tf_op jit(solution)/shard_map/all_to_all | solution.py:402
  151.9 0.2 convert_reduce_fusion
  152.1 1.1 broadcast_in_dim.7
  153.2 7.9 %all-to-all-start.4 = ((bf16[64,8,1152]{2,1,0:T(8,128)(2,1)}), bf16[64,8,1152]{2,1,0:T(8,128)(2,1)S(1)}, u32[]{:S(2)}, u32[]{:S(2)}) async-start(bf16[64,8,1152]{2,1,0:T(8,128)(2,1)} %broadcast_in_dim.7), calls=%async_computation.4 | async-start | bytes 2359296 | tf_op jit(solution)/shard_map/all_to_all | solution.py:402
  161.1 0.0 copy-start.2
  161.1 0.1 fusion.4
  161.2 1.1 copy-done.2
  162.3 1.6 pad_maximum_fusion
  163.9 13.7 %all-to-all-done.4 = bf16[64,8,1152]{2,1,0:T(8,128)(2,1)S(1)} async-done(((bf16[64,8,1152]{2,1,0:T(8,128)(2,1)}), bf16[64,8,1152]{2,1,0:T(8,128)(2,1)S(1)}, u32[]{:S(2)}, u32[]{:S(2)}) %all-to-all-start.4) | async-done | bytes 1179680 | tf_op jit(solution)/shard_map/all_to_all | solution.py:402
  177.6 3.5 %collective-permute-start.2 = (bf16[512,1152]{1,0:T(8,128)(2,1)S(1)}, bf16[512,1152]{1,0:T(8,128)(2,1)S(1)}, u32[]{:S(2)}, u32[]{:S(2)}) collective-permute-start(bf16[512,1152]{1,0:T(8,128)(2,1)S(1)} %bitcast.20), channel_id=1, source_target_pairs={{0,1},{1,0},{2,3},{3,2},{4,5},{5,4},{6,7},{7,6},{8,9},{9,8},{10,11... | collective-permute-start | bytes 3538952 | tf_op jit(solution)/shard_map/ppermute | solution.py:406
  181.0 0.1 convert_reduce_fusion.1
  181.1 0.6 slice_bitcast_fusion
  181.7 1.8 collective-permute-done.2.theirs_ref
  183.5 2.5 %join_halves.1 = (f32[512,1536]{1,0:T(8,128)}, f32[512,512]{1,0:T(8,128)}) custom-call(s32[1]{0:T(128)} %bitcast.refs_0_.core_ref, bf16[512,1152]{1,0:T(8,128)(2,1)S(1)} %bitcast.21, bf16[512,1152]{1,0:T(8,128)(2,1)S(1)} %collective-permute-done.2.theirs_ref), custom_call_target="tpu_custom_call" | custom-call | tf_op jit(solution)/shard_map/join_halves/pallas_call | solution.py:372
  (7 shorter events, 0.0 us)
Async XLA Ops:
  0.6 17.1 %copy-start = (f32[16,225]{1,0:T(8,128)S(1)}, f32[16,225]{1,0:T(8,128)}, u32[]{:S(2)}) copy-start(f32[16,225]{1,0:T(8,128)} %param.15) | copy-start | bytes 43204
  3.1 39.2 %all-to-all-start = ((bf16[64,32,512]{2,1,0:T(8,128)(2,1)}), bf16[64,32,512]{2,1,0:T(8,128)(2,1)S(1)}, u32[]{:S(2)}, u32[]{:S(2)}) async-start(bf16[64,32,512]{2,1,0:T(8,128)(2,1)} %pack_part.3), calls=%async_computation | async-start | bytes 4194304 | tf_op jit(solution)/shard_map/all_to_all | solution.py:402
  42.3 8.0 %copy-start.3 = (bf16[64,32,512]{2,1,0:T(8,128)(2,1)}, bf16[64,32,512]{2,1,0:T(8,128)(2,1)S(1)}, u32[]{:S(2)}) copy-start(bf16[64,32,512]{2,1,0:T(8,128)(2,1)S(1)} %all-to-all-done.refs_1_) | copy-start | bytes 6291460
  42.3 33.4 %all-to-all-start.1 = ((bf16[64,32,512]{2,1,0:T(8,128)(2,1)}), bf16[64,32,512]{2,1,0:T(8,128)(2,1)}, u32[]{:S(2)}, u32[]{:S(2)}) async-start(bf16[64,32,512]{2,1,0:T(8,128)(2,1)} %pack_part.2), calls=%async_computation.1 | async-start | bytes 4194304 | tf_op jit(solution)/shard_map/all_to_all | solution.py:402
  75.7 29.8 %all-to-all-start.2 = ((bf16[64,16,512]{2,1,0:T(8,128)(2,1)}), bf16[64,16,512]{2,1,0:T(8,128)(2,1)S(1)}, u32[]{:S(2)}, u32[]{:S(2)}) async-start(bf16[64,16,512]{2,1,0:T(8,128)(2,1)} %get-tuple-element.36), calls=%async_computation.2 | async-start | bytes 2097152 | tf_op jit(solution)/shard_map/all_to_all | solution.py:402
  105.6 8.2 %copy-start.1 = (bf16[64,16,512]{2,1,0:T(8,128)(2,1)}, bf16[64,16,512]{2,1,0:T(8,128)(2,1)S(1)}, u32[]{:S(2)}) copy-start(bf16[64,16,512]{2,1,0:T(8,128)(2,1)S(1)} %all-to-all-done.2) | copy-start | bytes 3145732
  105.6 5.6 %collective-permute-start = (bf16[512,1024]{1,0:T(8,128)(2,1)}, bf16[512,1024]{1,0:T(8,128)(2,1)S(1)}, u32[]{:S(2)}, u32[]{:S(2)}) collective-permute-start(bf16[512,1024]{1,0:T(8,128)(2,1)} %get-tuple-element.37), channel_id=1, source_target_pairs={{0,1},{1,0},{2,3},{3,2},{4,5},{5,4},{6,7},{7,6},{8,9},{9,8},{10,11... | collective-permute-start | bytes 3145736 | tf_op jit(solution)/shard_map/ppermute | solution.py:406
  113.8 10.1 %copy-start.4 = (f32[8,128]{1,0:T(8,128)S(1)}, f32[8,128]{1,0:T(8,128)}, u32[]{:S(2)}) copy-start(f32[8,128]{1,0:T(8,128)} %get-tuple-element.38) | copy-start | bytes 12292
  113.8 38.1 %all-to-all-start.3 = ((bf16[64,8,2048]{2,1,0:T(8,128)(2,1)}), bf16[64,8,2048]{2,1,0:T(8,128)(2,1)S(1)}, u32[]{:S(2)}, u32[]{:S(2)}) async-start(bf16[64,8,2048]{2,1,0:T(8,128)(2,1)} %fusion.2), calls=%async_computation.3 | async-start | bytes 4194304 | tf_op jit(solution)/shard_map/all_to_all | solution.py:402
  123.9 1.6 collective-permute-start.1
  153.2 24.4 %all-to-all-start.4 = ((bf16[64,8,1152]{2,1,0:T(8,128)(2,1)}), bf16[64,8,1152]{2,1,0:T(8,128)(2,1)S(1)}, u32[]{:S(2)}, u32[]{:S(2)}) async-start(bf16[64,8,1152]{2,1,0:T(8,128)(2,1)} %broadcast_in_dim.7), calls=%async_computation.4 | async-start | bytes 2359296 | tf_op jit(solution)/shard_map/all_to_all | solution.py:402
  161.1 1.2 copy-start.2
  177.6 5.9 %collective-permute-start.2 = (bf16[512,1152]{1,0:T(8,128)(2,1)S(1)}, bf16[512,1152]{1,0:T(8,128)(2,1)S(1)}, u32[]{:S(2)}, u32[]{:S(2)}) collective-permute-start(bf16[512,1152]{1,0:T(8,128)(2,1)S(1)} %bitcast.20), channel_id=1, source_target_pairs={{0,1},{1,0},{2,3},{3,2},{4,5},{5,4},{6,7},{7,6},{8,9},{9,8},{10,11... | collective-permute-start | bytes 3538952 | tf_op jit(solution)/shard_map/ppermute | solution.py:406

commit v4 on v3

--- a/solution.py
+++ b/solution.py
@@ -22,6 +22,7 @@
 CHUNKS = 4
 CHUNK = CELLS // CHUNKS
 VMEM_MIB = 60
+KERNEL_MIB = 44
 MIB = 1 << 20
 
 
@@ -109,23 +110,13 @@
         time += 1
 
 
-def copies_in(pairs, sems):
-    copies = [
-        pltpu.make_async_copy(source, target, sems.at[i])
-        for i, (source, target) in enumerate(pairs)
-    ]
-    for copy in copies:
-        copy.start()
-    return copies
-
-
 def chunk_copy(source, target, sems, c):
     part = pl.ds(c * CHUNK, CHUNK)
     return pltpu.make_async_copy(source.at[part], target.at[part], sems.at[c])
 
 
 def window_kernel(*refs, last):
-    core_ref, x_any, gain_ref, shift_ref, wqkv_any, wout_any, bias_any, mask_ref = refs[:8]
+    core_ref, x_any, gain_ref, shift_ref, wqkv_ref, wout_ref, bias_ref, mask_ref = refs[:8]
     refs = refs[8:]
     if last:
         gw_any, ln_in, out_any, other_any, ln_out = refs[:5]
@@ -134,18 +125,16 @@
     else:
         out_any, gw_any, ln_ref = refs[:3]
         refs = refs[3:]
-    x_ref, wqkv_ref, wout_ref, bias_ref, gw_ref, out_ref = refs[:6]
-    lat_slab, cot_slab, qkv, d_att, d_qkv, att, x_sems, sems, out_sems = refs[6:]
+    x_ref, gw_ref, out_ref = refs[:3]
+    lat_slab, cot_slab, qkv, d_att, d_qkv, att, x_sems, sems, out_sems = refs[3:]
     windows = x_ref.shape[1] // 2
 
     for c in range(CHUNKS):
         chunk_copy(x_any, x_ref, x_sems, c).start()
-    pairs = [(wout_any, wout_ref), (wqkv_any, wqkv_ref), (bias_any, bias_ref)]
     if last:
         ln_ref[...] = ln_in[...]
     else:
         ln_ref[...] = jnp.zeros_like(ln_ref)
-    loads = copies_in(pairs, sems)
     gw_ref[...] = jnp.zeros_like(gw_ref)
 
     def fill(c, carry):
@@ -160,8 +149,6 @@
         return carry
 
     lax.fori_loop(0, CHUNKS, fill, 0)
-    for load in loads:
-        load.wait()
     if last:
         before = pltpu.make_async_copy(gw_any, gw_before, sems.at[3])
         before.start()
@@ -254,7 +241,7 @@
     windows = x.shape[1] // 2
     cells = windows * CELLS
     shape = jax.ShapeDtypeStruct
-    everywhere = pl.BlockSpec(memory_space=pl.ANY)
+    hbm = pl.BlockSpec(memory_space=pltpu.HBM)
     vmem = pl.BlockSpec(memory_space=pltpu.VMEM)
     grads = shape((4, 512, 512), F32)
     ln = shape((2, 8, 512), F32)
@@ -270,16 +257,13 @@
         kernel,
         in_specs=[
             pl.BlockSpec(memory_space=pltpu.SMEM),
-            everywhere, vmem, vmem, everywhere, everywhere, everywhere, vmem,
+            hbm, vmem, vmem, vmem, vmem, vmem, vmem,
         ]
-        + ([everywhere, vmem] if last else []),
-        out_specs=[everywhere, everywhere, vmem],
+        + ([hbm, vmem] if last else []),
+        out_specs=[hbm, hbm, vmem],
         out_shape=outs,
         scratch_shapes=[
             pltpu.VMEM(x.shape, BF16),
-            pltpu.VMEM(w_qkv.shape, BF16),
-            pltpu.VMEM(w_out.shape, BF16),
-            pltpu.VMEM(bias.shape, F32),
             pltpu.VMEM(grads.shape, F32),
             pltpu.VMEM(outs[0].shape, BF16),
             pltpu.VMEM((4, cells, 128), F32),
@@ -301,12 +285,36 @@
             if last
             else []
         ),
-        compiler_params=pltpu.CompilerParams(vmem_limit_bytes=VMEM_MIB * MIB),
+        compiler_params=pltpu.CompilerParams(vmem_limit_bytes=KERNEL_MIB * MIB),
         cost_estimate=pl.CostEstimate(
             flops=20 * 10**9, bytes_accessed=12 * MIB, transcendentals=10**6
         ),
         name="window_last" if last else "window_first",
     )(core, x, gain, shift, w_qkv, w_out, bias, mask, *(sums or ()))
+
+
+def stage(*arrays):
+    def kernel(*refs):
+        count = len(arrays)
+        sems = refs[-1]
+        copies = [
+            pltpu.make_async_copy(refs[i], refs[count + i], sems.at[i]) for i in range(count)
+        ]
+        for copy in copies:
+            copy.start()
+        for copy in copies:
+            copy.wait()
+
+    return pl.pallas_call(
+        kernel,
+        in_specs=[pl.BlockSpec(memory_space=pltpu.HBM)] * len(arrays),
+        out_specs=[pl.BlockSpec(memory_space=pltpu.VMEM)] * len(arrays),
+        out_shape=[jax.ShapeDtypeStruct(a.shape, a.dtype) for a in arrays],
+        scratch_shapes=[pltpu.SemaphoreType.DMA((len(arrays),))],
+        compiler_params=pltpu.CompilerParams(vmem_limit_bytes=KERNEL_MIB * MIB),
+        cost_estimate=pl.CostEstimate(flops=0, bytes_accessed=3 * MIB, transcendentals=0),
+        name="stage_constants",
+    )(*arrays)
 
 
 def pack(latent, cotangent, part, half):
@@ -338,11 +346,11 @@
         for c in range(pieces):
             store(c).wait()
 
-    everywhere = pl.BlockSpec(memory_space=pl.ANY)
+    hbm = pl.BlockSpec(memory_space=pltpu.HBM)
     return pl.pallas_call(
         kernel,
-        in_specs=[everywhere, everywhere],
-        out_specs=everywhere,
+        in_specs=[hbm, hbm],
+        out_specs=hbm,
         out_shape=jax.ShapeDtypeStruct((peers, 2 * half, width), BF16),
         scratch_shapes=[
             pltpu.VMEM((peers, 2 * half, width), BF16),
@@ -421,6 +429,7 @@
         (4, CELLS, 128),
     )
     bias = bias_tables(rel_bias)
+    w_qkv, w_out, bias, mask = stage(w_qkv, w_out, bias, mask)
     consts = (gain, shift, w_qkv, w_out, bias, mask)
     core_id = core.astype(jnp.int32).reshape(1)
 

time: 187 us -> 186 us (level)
  Pallas kernels: 47.9 us -> 43.4 us
  local copies, waits for them, and re-layouts: 5.25 us -> 8.91 us
  waiting for transfers between devices: 71.8 us -> 69.9 us
    unnamed x10 -> x20, local copies, waits for them, and re-layouts: 1.15 us -> 6.15 us
    pallas_call x4 -> x5, Pallas kernels: 45.4 us -> 40.9 us  [the longest x2 35.7 us: window_pass(): pl.pallas_call(kernel, in_specs=[pl.BlockSpec(memory_space=pltpu.SMEM), h...]
  transfers between devices with their start and end apart: 8 -> 8, of which waited for: 7 -> 7; matrix products, arithmetic and copies ran while one was open for 3% -> 3% of each run, Pallas kernels for 23% -> 21%
where the time goes in v4:
time: 186 us; the launch traced here: 185 us
  waiting for transfers between devices  69.9 us (38%)
  starting transfers between devices  54.7 us (29%)
  Pallas kernels  43.4 us (23%)
  local copies, waits for them, and re-layouts  8.91 us (5%)
  other arithmetic  5.76 us (3%)
    all_to_all x5, waiting for transfers between devices, exchange(): lax.all_to_all(array, ('gx', 'gh'), split_axis=0, concat_axis=0, tiled=True)  65 us
    all_to_all x5, starting transfers between devices, exchange(): lax.all_to_all(array, ('gx', 'gh'), split_axis=0, concat_axis=0, tiled=True)  47.4 us
    pallas_call x2, Pallas kernels, window_pass(): pl.pallas_call(kernel, in_specs=[pl.BlockSpec(memory_space=pltpu.SMEM), h...  35.7 us
    ppermute x3, starting transfers between devices, swap_cores(): return lax.ppermute(array, 'core', [(0, 1), (1, 0)])  7.28 us
    unnamed x20, local copies, waits for them, and re-layouts  6.15 us
    ppermute x3, waiting for transfers between devices, swap_cores(): return lax.ppermute(array, 'core', [(0, 1), (1, 0)])  4.92 us
    pallas_call x2, Pallas kernels, pack(): pl.pallas_call(kernel, in_specs=[hbm, hbm], out_specs=hbm, out_shape=jax....  4.9 us
  transfers between devices with their start and end apart: 8, of which 7 were waited for; matrix products, arithmetic and copies ran while one was open for 3% of the time, Pallas kernels for 21%

profile of v4, /device:TPU:1, one launch (start us, length us, event | category | flops | bytes accessed | tf_op | source)
XLA Modules:
  0.0 184.9 jit_solution(9150869952938004675)
XLA Ops:
  0.6 0.0 copy-start
  0.6 2.4 %pack_part.3 = bf16[64,32,512]{2,1,0:T(8,128)(2,1)} custom-call(bf16[64,32,512]{2,1,0:T(8,128)(2,1)} %bitcast.26, bf16[64,32,512]{2,1,0:T(8,128)(2,1)} %bitcast.28), custom_call_target="tpu_custom_call" | custom-call | bytes 4194304 | tf_op jit(solution)/shard_map/pack_part/pallas_call | solution.py:350
  3.1 12.0 %all-to-all-start = ((bf16[64,32,512]{2,1,0:T(8,128)(2,1)}), bf16[64,32,512]{2,1,0:T(8,128)(2,1)S(1)}, u32[]{:S(2)}, u32[]{:S(2)}) async-start(bf16[64,32,512]{2,1,0:T(8,128)(2,1)} %pack_part.3), calls=%async_computation | async-start | bytes 4194304 | tf_op jit(solution)/shard_map/all_to_all | solution.py:410
  15.1 2.4 %pack_part.2 = bf16[64,32,512]{2,1,0:T(8,128)(2,1)} custom-call(bf16[64,32,512]{2,1,0:T(8,128)(2,1)} %bitcast.27, bf16[64,32,512]{2,1,0:T(8,128)(2,1)} %bitcast.29), custom_call_target="tpu_custom_call" | custom-call | bytes 4194304 | tf_op jit(solution)/shard_map/pack_part/pallas_call | solution.py:350
  17.6 0.1 add_add_fusion
  17.6 0.1 add.66
  17.7 1.3 convolution_bitcast_fusion
  19.1 0.2 reshape.216
  19.3 0.3 copy.14
  19.6 0.3 reshape.217.refs_2_
  20.0 0.0 copy-start.2
  20.0 22.3 %all-to-all-done.refs_1_ = bf16[64,32,512]{2,1,0:T(8,128)(2,1)S(1)} async-done(((bf16[64,32,512]{2,1,0:T(8,128)(2,1)}), bf16[64,32,512]{2,1,0:T(8,128)(2,1)S(1)}, u32[]{:S(2)}, u32[]{:S(2)}) %all-to-all-start) | async-done | bytes 2097184 | tf_op jit(solution)/shard_map/all_to_all | solution.py:410
  42.3 8.0 %all-to-all-start.1 = ((bf16[64,32,512]{2,1,0:T(8,128)(2,1)}), bf16[64,32,512]{2,1,0:T(8,128)(2,1)}, u32[]{:S(2)}, u32[]{:S(2)}) async-start(bf16[64,32,512]{2,1,0:T(8,128)(2,1)} %pack_part.2), calls=%async_computation.1 | async-start | bytes 4194304 | tf_op jit(solution)/shard_map/all_to_all | solution.py:410
  50.3 0.0 copy-start.7
  50.3 0.0 copy-start.8
  50.4 0.0 copy-start.1
  50.4 1.4 copy-done.1
  51.8 0.3 stage_constants.1
  52.1 17.2 %window_first.1 = (bf16[64,16,512]{2,1,0:T(8,128)(2,1)}, f32[4,512,512]{2,1,0:T(8,128)S(1)}, f32[2,8,512]{2,1,0:T(8,128)S(1)}) custom-call(s32[1]{0:T(128)} %bitcast.refs_0_.core_ref, bf16[64,32,512]{2,1,0:T(8,128)(2,1)S(1)} %all-to-all-done.refs_1_, f32[1,512]{1,0:T(1,128)S(1)} %bitcast.22, f32[1,512]{1,0:T(1,128)S(1)} %bitcast.24, ...), custom_call_target="tpu_custom_call" | custom-call | flops 20000000000 | bytes 12582912 | tf_op jit(solution)/shard_map/window_first/pallas_call | solution.py:256
  69.4 0.0 copy-start.3
  69.4 1.1 copy-done.3
  70.5 0.7 copy-done.5
  71.2 1.9 %copy-done.9 = f32[4,512,512]{2,1,0:T(8,128)} copy-done((f32[4,512,512]{2,1,0:T(8,128)}, f32[4,512,512]{2,1,0:T(8,128)S(1)}, u32[]{:S(2)}) %copy-start.9) | copy-done | bytes 4194328
  73.1 2.6 %all-to-all-done.1.refs_1_ = bf16[64,32,512]{2,1,0:T(8,128)(2,1)} async-done(((bf16[64,32,512]{2,1,0:T(8,128)(2,1)}), bf16[64,32,512]{2,1,0:T(8,128)(2,1)}, u32[]{:S(2)}, u32[]{:S(2)}) %all-to-all-start.1) | async-done | bytes 2097184 | tf_op jit(solution)/shard_map/all_to_all | solution.py:410
  75.7 9.5 %all-to-all-start.2 = ((bf16[64,16,512]{2,1,0:T(8,128)(2,1)}), bf16[64,16,512]{2,1,0:T(8,128)(2,1)}, u32[]{:S(2)}, u32[]{:S(2)}) async-start(bf16[64,16,512]{2,1,0:T(8,128)(2,1)} %get-tuple-element.44), calls=%async_computation.2 | async-start | bytes 2097152 | tf_op jit(solution)/shard_map/all_to_all | solution.py:410
  85.2 0.0 copy-done.4
  85.2 0.0 copy-start.6
  85.3 0.9 copy-done.6
  86.2 18.5 %window_last.1 = (bf16[64,8,2048]{2,1,0:T(8,128)(2,1)}, bf16[512,1024]{1,0:T(8,128)(2,1)S(1)}, f32[8,128]{1,0:T(8,128)S(1)}) custom-call(s32[1]{0:T(128)} %bitcast.refs_0_.core_ref, bf16[64,32,512]{2,1,0:T(8,128)(2,1)} %all-to-all-done.1.refs_1_, f32[1,512]{1,0:T(1,128)S(1)} %bitcast.23, f32[1,512]{1,0:T(1,128)S(1)} %bitcast.25, ...), custom_call_target="tpu_custom_call" | custom-call | flops 20000000000 | bytes 12582912 | tf_op jit(solution)/shard_map/window_last/pallas_call | solution.py:256
  104.7 0.0 all-to-all-done.2
  104.7 3.1 %collective-permute-start = (bf16[512,1024]{1,0:T(8,128)(2,1)S(1)}, bf16[512,1024]{1,0:T(8,128)(2,1)S(1)}, u32[]{:S(2)}, u32[]{:S(2)}) collective-permute-start(bf16[512,1024]{1,0:T(8,128)(2,1)S(1)} %get-tuple-element.45), channel_id=1, source_target_pairs={{0,1},{1,0},{2,3},{3,2},{4,5},{5,4},{6,7},{7,6},{8,9},{9,8},{10,11... | collective-permute-start | bytes 3145736 | tf_op jit(solution)/shard_map/ppermute | solution.py:414
  107.8 2.3 %collective-permute-done = bf16[512,1024]{1,0:T(8,128)(2,1)S(1)} collective-permute-done((bf16[512,1024]{1,0:T(8,128)(2,1)S(1)}, bf16[512,1024]{1,0:T(8,128)(2,1)S(1)}, u32[]{:S(2)}, u32[]{:S(2)}) %collective-permute-start) | collective-permute-done | bytes 1048608 | tf_op jit(solution)/shard_map/ppermute | solution.py:414
  110.1 2.6 %fusion.2 = bf16[64,8,2048]{2,1,0:T(8,128)(2,1)} fusion(bf16[64,8,2048]{2,1,0:T(8,128)(2,1)} %get-tuple-element.41, bf16[512,1024]{1,0:T(8,128)(2,1)S(1)} %collective-permute-done), kind=kLoop, calls=%fused_computation.7 | loop fusion | flops 2097152 | bytes 3145728 | tf_op jit(solution)/shard_map/scatter | solution.py:448
  112.7 10.0 %all-to-all-start.3 = ((bf16[64,8,2048]{2,1,0:T(8,128)(2,1)}), bf16[64,8,2048]{2,1,0:T(8,128)(2,1)S(1)}, u32[]{:S(2)}, u32[]{:S(2)}) async-start(bf16[64,8,2048]{2,1,0:T(8,128)(2,1)} %fusion.2), calls=%async_computation.3 | async-start | bytes 4194304 | tf_op jit(solution)/shard_map/all_to_all | solution.py:410
  122.8 0.7 collective-permute-start.1
  123.5 0.8 collective-permute-done.1
  124.3 26.4 %all-to-all-done.3 = bf16[64,8,2048]{2,1,0:T(8,128)(2,1)S(1)} async-done(((bf16[64,8,2048]{2,1,0:T(8,128)(2,1)}), bf16[64,8,2048]{2,1,0:T(8,128)(2,1)S(1)}, u32[]{:S(2)}, u32[]{:S(2)}) %all-to-all-start.3) | async-done | bytes 2097184 | tf_op jit(solution)/shard_map/all_to_all | solution.py:410
  150.8 0.2 convert_reduce_fusion
  150.9 1.1 broadcast_in_dim.5
  152.0 7.9 %all-to-all-start.4 = ((bf16[64,8,1152]{2,1,0:T(8,128)(2,1)}), bf16[64,8,1152]{2,1,0:T(8,128)(2,1)S(1)}, u32[]{:S(2)}, u32[]{:S(2)}) async-start(bf16[64,8,1152]{2,1,0:T(8,128)(2,1)} %broadcast_in_dim.5), calls=%async_computation.4 | async-start | bytes 2359296 | tf_op jit(solution)/shard_map/all_to_all | solution.py:410
  159.9 0.1 fusion.4
  160.0 2.8 %pad_maximum_fusion = bf16[64,32,512]{2,1,0:T(8,128)(2,1)} fusion(bf16[64,8,512]{2,1,0:T(8,128)(2,1)S(1)} %get-tuple-element.52, bf16[64,8,512]{2,1,0:T(8,128)(2,1)S(1)} %get-tuple-element.51, bf16[64,16,512]{2,1,0:T(8,128)(2,1)} %all-to-all-done.2), kind=kLoop, calls=%fused_computation.2 | loop fusion | flops 6291456 | bytes 4194304 | tf_op jit(solution)/shard_map/concatenate | solution.py:452
  162.8 13.6 %all-to-all-done.4 = bf16[64,8,1152]{2,1,0:T(8,128)(2,1)S(1)} async-done(((bf16[64,8,1152]{2,1,0:T(8,128)(2,1)}), bf16[64,8,1152]{2,1,0:T(8,128)(2,1)S(1)}, u32[]{:S(2)}, u32[]{:S(2)}) %all-to-all-start.4) | async-done | bytes 1179680 | tf_op jit(solution)/shard_map/all_to_all | solution.py:410
  176.4 3.5 %collective-permute-start.2 = (bf16[512,1152]{1,0:T(8,128)(2,1)S(1)}, bf16[512,1152]{1,0:T(8,128)(2,1)S(1)}, u32[]{:S(2)}, u32[]{:S(2)}) collective-permute-start(bf16[512,1152]{1,0:T(8,128)(2,1)S(1)} %bitcast.20), channel_id=1, source_target_pairs={{0,1},{1,0},{2,3},{3,2},{4,5},{5,4},{6,7},{7,6},{8,9},{9,8},{10,11... | collective-permute-start | bytes 3538952 | tf_op jit(solution)/shard_map/ppermute | solution.py:414
  179.9 0.1 convert_reduce_fusion.1
  180.0 0.6 slice_bitcast_fusion
  180.6 1.8 collective-permute-done.2.theirs_ref
  182.4 2.5 %join_halves.1 = (f32[512,1536]{1,0:T(8,128)}, f32[512,512]{1,0:T(8,128)}) custom-call(s32[1]{0:T(128)} %bitcast.refs_0_.core_ref, bf16[512,1152]{1,0:T(8,128)(2,1)S(1)} %bitcast.21, bf16[512,1152]{1,0:T(8,128)(2,1)S(1)} %collective-permute-done.2.theirs_ref), custom_call_target="tpu_custom_call" | custom-call | tf_op jit(solution)/shard_map/join_halves/pallas_call | solution.py:380
  (15 shorter events, 0.1 us)
Async XLA Ops:
  0.6 17.1 %copy-start = (f32[16,225]{1,0:T(8,128)S(1)}, f32[16,225]{1,0:T(8,128)}, u32[]{:S(2)}) copy-start(f32[16,225]{1,0:T(8,128)} %param.15) | copy-start | bytes 43204
  3.1 39.2 %all-to-all-start = ((bf16[64,32,512]{2,1,0:T(8,128)(2,1)}), bf16[64,32,512]{2,1,0:T(8,128)(2,1)S(1)}, u32[]{:S(2)}, u32[]{:S(2)}) async-start(bf16[64,32,512]{2,1,0:T(8,128)(2,1)} %pack_part.3), calls=%async_computation | async-start | bytes 4194304 | tf_op jit(solution)/shard_map/all_to_all | solution.py:410
  20.0 30.4 %copy-start.2 = (bf16[512,512]{1,0:T(8,128)(2,1)S(1)}, bf16[512,512]{1,0:T(8,128)(2,1)}, u32[]{:S(2)}) copy-start(bf16[512,512]{1,0:T(8,128)(2,1)} %refs_1_.1) | copy-start | bytes 1572868
  42.3 33.4 %all-to-all-start.1 = ((bf16[64,32,512]{2,1,0:T(8,128)(2,1)}), bf16[64,32,512]{2,1,0:T(8,128)(2,1)}, u32[]{:S(2)}, u32[]{:S(2)}) async-start(bf16[64,32,512]{2,1,0:T(8,128)(2,1)} %pack_part.2), calls=%async_computation.1 | async-start | bytes 4194304 | tf_op jit(solution)/shard_map/all_to_all | solution.py:410
  50.3 1.8 copy-start.7
  50.3 1.8 copy-start.8
  50.4 1.4 copy-start.1
  69.4 1.1 copy-start.3
  70.5 0.7 copy-start.5
  71.2 1.9 %copy-start.9 = (f32[4,512,512]{2,1,0:T(8,128)}, f32[4,512,512]{2,1,0:T(8,128)S(1)}, u32[]{:S(2)}) copy-start(f32[4,512,512]{2,1,0:T(8,128)S(1)} %get-tuple-element.39.refs_8_) | copy-start | bytes 12582916
  75.7 9.5 %copy-start.4 = (bf16[512,1536]{1,0:T(8,128)(2,1)S(1)}, bf16[512,1536]{1,0:T(8,128)(2,1)}, u32[]{:S(2)}) copy-start(bf16[512,1536]{1,0:T(8,128)(2,1)} %copy-done.3) | copy-start | bytes 4718596
  75.7 29.0 %all-to-all-start.2 = ((bf16[64,16,512]{2,1,0:T(8,128)(2,1)}), bf16[64,16,512]{2,1,0:T(8,128)(2,1)}, u32[]{:S(2)}, u32[]{:S(2)}) async-start(bf16[64,16,512]{2,1,0:T(8,128)(2,1)} %get-tuple-element.44), calls=%async_computation.2 | async-start | bytes 2097152 | tf_op jit(solution)/shard_map/all_to_all | solution.py:410
  85.2 1.0 copy-start.6
  104.7 5.4 %collective-permute-start = (bf16[512,1024]{1,0:T(8,128)(2,1)S(1)}, bf16[512,1024]{1,0:T(8,128)(2,1)S(1)}, u32[]{:S(2)}, u32[]{:S(2)}) collective-permute-start(bf16[512,1024]{1,0:T(8,128)(2,1)S(1)} %get-tuple-element.45), channel_id=1, source_target_pairs={{0,1},{1,0},{2,3},{3,2},{4,5},{5,4},{6,7},{7,6},{8,9},{9,8},{10,11... | collective-permute-start | bytes 3145736 | tf_op jit(solution)/shard_map/ppermute | solution.py:414
  112.7 38.1 %all-to-all-start.3 = ((bf16[64,8,2048]{2,1,0:T(8,128)(2,1)}), bf16[64,8,2048]{2,1,0:T(8,128)(2,1)S(1)}, u32[]{:S(2)}, u32[]{:S(2)}) async-start(bf16[64,8,2048]{2,1,0:T(8,128)(2,1)} %fusion.2), calls=%async_computation.3 | async-start | bytes 4194304 | tf_op jit(solution)/shard_map/all_to_all | solution.py:410
  122.8 1.6 collective-permute-start.1
  152.0 24.4 %all-to-all-start.4 = ((bf16[64,8,1152]{2,1,0:T(8,128)(2,1)}), bf16[64,8,1152]{2,1,0:T(8,128)(2,1)S(1)}, u32[]{:S(2)}, u32[]{:S(2)}) async-start(bf16[64,8,1152]{2,1,0:T(8,128)(2,1)} %broadcast_in_dim.5), calls=%async_computation.4 | async-start | bytes 2359296 | tf_op jit(solution)/shard_map/all_to_all | solution.py:410
  176.4 5.9 %collective-permute-start.2 = (bf16[512,1152]{1,0:T(8,128)(2,1)S(1)}, bf16[512,1152]{1,0:T(8,128)(2,1)S(1)}, u32[]{:S(2)}, u32[]{:S(2)}) collective-permute-start(bf16[512,1152]{1,0:T(8,128)(2,1)S(1)} %bitcast.20), channel_id=1, source_target_pairs={{0,1},{1,0},{2,3},{3,2},{4,5},{5,4},{6,7},{7,6},{8,9},{9,8},{10,11... | collective-permute-start | bytes 3538952 | tf_op jit(solution)/shard_map/ppermute | solution.py:414

commit v5 on v4

--- a/solution.py
+++ b/solution.py
@@ -363,32 +363,75 @@
     )(latent, cotangent)
 
 
-def join_kernel(core_ref, ours_ref, theirs_ref, gq_ref, go_ref):
-    own = core_ref[0] == 0
-    ours = ours_ref[:, :1024].astype(F32)
-    theirs = theirs_ref[:, :1024].astype(F32)
-    gq_ref[:, :1024] = jnp.where(own, ours, theirs)
-    high = jnp.where(own, theirs, ours)
-    gq_ref[:, 1024:] = high[:, :512]
-    go_ref[...] = high[:, 512:]
-
-
-def join(core, ours, theirs):
-    def block(width):
-        return pl.BlockSpec((128, width), lambda i: (i, 0))
+def place_kernel(core_ref, half_ref, *refs, own):
+    gq_any, go_any, wide, sems = refs[-4:]
+    low = core_ref[0] == (0 if own else 1)
+    pieces = 4
+    size = wide.shape[0] // pieces
+
+    def copies(p):
+        rows = pl.ds(p * size, size)
+        first = pltpu.make_async_copy(
+            wide.at[rows], gq_any.at[rows, pl.ds(0, 1024)], sems.at[p]
+        )
+        second = pltpu.make_async_copy(
+            wide.at[rows, pl.ds(0, 512)], gq_any.at[rows, pl.ds(1024, 512)], sems.at[p]
+        )
+        third = pltpu.make_async_copy(
+            wide.at[rows, pl.ds(512, 512)], go_any.at[rows], sems.at[pieces + p]
+        )
+        return first, second, third
+
+    for p in range(pieces):
+        rows = pl.ds(p * size, size)
+        wide[rows, :] = half_ref[rows, :1024].astype(F32)
+
+        @pl.when(low)
+        def _():
+            copies(p)[0].start()
+
+        @pl.when(jnp.logical_not(low))
+        def _():
+            copies(p)[1].start()
+            copies(p)[2].start()
+
+    for p in range(pieces):
+
+        @pl.when(low)
+        def _():
+            copies(p)[0].wait()
+
+        @pl.when(jnp.logical_not(low))
+        def _():
+            copies(p)[1].wait()
+            copies(p)[2].wait()
+
+
+def place(core, half, placed):
+    own = placed is None
+    hbm = pl.BlockSpec(memory_space=pltpu.HBM)
+
+    def kernel(*refs):
+        place_kernel(*refs, own=own)
 
     return pl.pallas_call(
-        join_kernel,
-        grid=(4,),
-        in_specs=[pl.BlockSpec(memory_space=pltpu.SMEM), block(1152), block(1152)],
-        out_specs=[block(1536), block(512)],
+        kernel,
+        in_specs=[
+            pl.BlockSpec(memory_space=pltpu.SMEM),
+            pl.BlockSpec(memory_space=pltpu.VMEM),
+        ]
+        + ([] if own else [hbm, hbm]),
+        out_specs=[hbm, hbm],
         out_shape=[
             jax.ShapeDtypeStruct((512, 1536), F32),
             jax.ShapeDtypeStruct((512, 512), F32),
         ],
-        compiler_params=pltpu.CompilerParams(vmem_limit_bytes=8 * MIB),
-        name="join_halves",
-    )(core, ours, theirs)
+        scratch_shapes=[pltpu.VMEM((512, 1024), F32), pltpu.SemaphoreType.DMA((8,))],
+        input_output_aliases={} if own else {2: 0, 3: 1},
+        compiler_params=pltpu.CompilerParams(vmem_limit_bytes=16 * MIB),
+        cost_estimate=pl.CostEstimate(flops=0, bytes_accessed=3 * MIB, transcendentals=0),
+        name="place_own" if own else "place_other",
+    )(core, half, *(placed or ()))
 
 
 def bias_tables(rel_bias):
@@ -454,7 +497,9 @@
     )
     full, result = lax.optimization_barrier((full, result))
     ours = full.reshape(width, 1152)
-    grad_qkv, grad_out = join(core_id, ours, swap_cores(ours))
+    theirs = swap_cores(ours)
+    placed = place(core_id, ours, None)
+    grad_qkv, grad_out = place(core_id, theirs, placed)
     ln_total = (jnp.sum(full[:, :, 1024:].astype(F32), axis=0) * norm).reshape(2, width)
     return (result.reshape(rows, cols, width), grad_qkv, grad_out, ln_total[0], ln_total[1])
 

time: 186 us -> 185 us (level)
  transfers between devices with their start and end apart: 8 -> 8, of which waited for: 7 -> 7; matrix products, arithmetic and copies ran while one was open for 3% -> 3% of each run, Pallas kernels for 21% -> 22%
where the time goes in v5:
time: 185 us; the launch traced here: 184 us
  waiting for transfers between devices  68.5 us (37%)
  starting transfers between devices  54.7 us (30%)
  Pallas kernels  43.7 us (24%)
  local copies, waits for them, and re-layouts  8.91 us (5%)
  other arithmetic  5.76 us (3%)
    all_to_all x5, waiting for transfers between devices, exchange(): lax.all_to_all(array, ('gx', 'gh'), split_axis=0, concat_axis=0, tiled=True)  65 us
    all_to_all x5, starting transfers between devices, exchange(): lax.all_to_all(array, ('gx', 'gh'), split_axis=0, concat_axis=0, tiled=True)  47.4 us
    pallas_call x2, Pallas kernels, window_pass(): pl.pallas_call(kernel, in_specs=[pl.BlockSpec(memory_space=pltpu.SMEM), h...  35.7 us
    ppermute x3, starting transfers between devices, swap_cores(): return lax.ppermute(array, 'core', [(0, 1), (1, 0)])  7.28 us
    unnamed x20, local copies, waits for them, and re-layouts  6.15 us
    pallas_call x2, Pallas kernels, pack(): pl.pallas_call(kernel, in_specs=[hbm, hbm], out_specs=hbm, out_shape=jax....  4.9 us
  transfers between devices with their start and end apart: 8, of which 7 were waited for; matrix products, arithmetic and copies ran while one was open for 3% of the time, Pallas kernels for 22%

profile of v5, /device:TPU:1, one launch (start us, length us, event | category | flops | bytes accessed | tf_op | source)
XLA Modules:
  0.0 184.0 jit_solution(3864693259602549242)
XLA Ops:
  0.6 0.0 copy-start
  0.6 2.4 %pack_part.3 = bf16[64,32,512]{2,1,0:T(8,128)(2,1)} custom-call(bf16[64,32,512]{2,1,0:T(8,128)(2,1)} %bitcast.26, bf16[64,32,512]{2,1,0:T(8,128)(2,1)} %bitcast.28), custom_call_target="tpu_custom_call" | custom-call | bytes 4194304 | tf_op jit(solution)/shard_map/pack_part/pallas_call | solution.py:350
  3.1 12.0 %all-to-all-start = ((bf16[64,32,512]{2,1,0:T(8,128)(2,1)}), bf16[64,32,512]{2,1,0:T(8,128)(2,1)S(1)}, u32[]{:S(2)}, u32[]{:S(2)}) async-start(bf16[64,32,512]{2,1,0:T(8,128)(2,1)} %pack_part.3), calls=%async_computation | async-start | bytes 4194304 | tf_op jit(solution)/shard_map/all_to_all | solution.py:453
  15.1 2.4 %pack_part.2 = bf16[64,32,512]{2,1,0:T(8,128)(2,1)} custom-call(bf16[64,32,512]{2,1,0:T(8,128)(2,1)} %bitcast.27, bf16[64,32,512]{2,1,0:T(8,128)(2,1)} %bitcast.29), custom_call_target="tpu_custom_call" | custom-call | bytes 4194304 | tf_op jit(solution)/shard_map/pack_part/pallas_call | solution.py:350
  17.6 0.1 add_add_fusion
  17.6 0.1 add.66
  17.7 0.0 copy-done
  17.7 1.3 convolution_bitcast_fusion
  19.1 0.2 reshape.216
  19.3 0.3 copy.16
  19.6 0.3 reshape.217.refs_2_
  20.0 0.0 copy-start.2
  20.0 22.3 %all-to-all-done.refs_1_ = bf16[64,32,512]{2,1,0:T(8,128)(2,1)S(1)} async-done(((bf16[64,32,512]{2,1,0:T(8,128)(2,1)}), bf16[64,32,512]{2,1,0:T(8,128)(2,1)S(1)}, u32[]{:S(2)}, u32[]{:S(2)}) %all-to-all-start) | async-done | bytes 2097184 | tf_op jit(solution)/shard_map/all_to_all | solution.py:453
  42.3 8.0 %all-to-all-start.1 = ((bf16[64,32,512]{2,1,0:T(8,128)(2,1)}), bf16[64,32,512]{2,1,0:T(8,128)(2,1)}, u32[]{:S(2)}, u32[]{:S(2)}) async-start(bf16[64,32,512]{2,1,0:T(8,128)(2,1)} %pack_part.2), calls=%async_computation.1 | async-start | bytes 4194304 | tf_op jit(solution)/shard_map/all_to_all | solution.py:453
  50.3 0.0 copy-start.7
  50.3 0.0 copy-start.8
  50.4 0.0 copy-start.1
  50.4 1.4 copy-done.1
  51.8 0.3 stage_constants.1
  52.1 17.2 %window_first.1 = (bf16[64,16,512]{2,1,0:T(8,128)(2,1)}, f32[4,512,512]{2,1,0:T(8,128)S(1)}, f32[2,8,512]{2,1,0:T(8,128)S(1)}) custom-call(s32[1]{0:T(128)} %bitcast.refs_0_, bf16[64,32,512]{2,1,0:T(8,128)(2,1)S(1)} %all-to-all-done.refs_1_, f32[1,512]{1,0:T(1,128)S(1)} %bitcast.22, f32[1,512]{1,0:T(1,128)S(1)} %bitcast.24, ...), custom_call_target="tpu_custom_call" | custom-call | flops 20000000000 | bytes 12582912 | tf_op jit(solution)/shard_map/window_first/pallas_call | solution.py:256
  69.4 0.0 copy-start.3
  69.4 1.1 copy-done.3
  70.5 0.7 copy-done.5
  71.2 1.9 %copy-done.9 = f32[4,512,512]{2,1,0:T(8,128)} copy-done((f32[4,512,512]{2,1,0:T(8,128)}, f32[4,512,512]{2,1,0:T(8,128)S(1)}, u32[]{:S(2)}) %copy-start.9) | copy-done | bytes 4194328
  73.1 2.6 %all-to-all-done.1.refs_1_ = bf16[64,32,512]{2,1,0:T(8,128)(2,1)} async-done(((bf16[64,32,512]{2,1,0:T(8,128)(2,1)}), bf16[64,32,512]{2,1,0:T(8,128)(2,1)}, u32[]{:S(2)}, u32[]{:S(2)}) %all-to-all-start.1) | async-done | bytes 2097184 | tf_op jit(solution)/shard_map/all_to_all | solution.py:453
  75.7 9.5 %all-to-all-start.2 = ((bf16[64,16,512]{2,1,0:T(8,128)(2,1)}), bf16[64,16,512]{2,1,0:T(8,128)(2,1)}, u32[]{:S(2)}, u32[]{:S(2)}) async-start(bf16[64,16,512]{2,1,0:T(8,128)(2,1)} %get-tuple-element.46), calls=%async_computation.2 | async-start | bytes 2097152 | tf_op jit(solution)/shard_map/all_to_all | solution.py:453
  85.3 0.9 copy-done.6
  86.2 18.5 %window_last.1 = (bf16[64,8,2048]{2,1,0:T(8,128)(2,1)}, bf16[512,1024]{1,0:T(8,128)(2,1)S(1)}, f32[8,128]{1,0:T(8,128)S(1)}) custom-call(s32[1]{0:T(128)} %bitcast.refs_0_, bf16[64,32,512]{2,1,0:T(8,128)(2,1)} %all-to-all-done.1.refs_1_, f32[1,512]{1,0:T(1,128)S(1)} %bitcast.23, f32[1,512]{1,0:T(1,128)S(1)} %bitcast.25, bf16[512,1536]{1,0:T(8,128)(2,1)S(1)} %copy-done.4, ...), custom_call_target="tpu_custom_call" | custom-call | flops 20000000000 | bytes 12582912 | tf_op jit(solution)/shard_map/window_last/pallas_call | solution.py:256
  104.7 0.0 all-to-all-done.2
  104.7 3.1 %collective-permute-start = (bf16[512,1024]{1,0:T(8,128)(2,1)S(1)}, bf16[512,1024]{1,0:T(8,128)(2,1)S(1)}, u32[]{:S(2)}, u32[]{:S(2)}) collective-permute-start(bf16[512,1024]{1,0:T(8,128)(2,1)S(1)} %get-tuple-element.47), channel_id=1, source_target_pairs={{0,1},{1,0},{2,3},{3,2},{4,5},{5,4},{6,7},{7,6},{8,9},{9,8},{10,11... | collective-permute-start | bytes 3145736 | tf_op jit(solution)/shard_map/ppermute | solution.py:457
  107.8 2.3 %collective-permute-done = bf16[512,1024]{1,0:T(8,128)(2,1)S(1)} collective-permute-done((bf16[512,1024]{1,0:T(8,128)(2,1)S(1)}, bf16[512,1024]{1,0:T(8,128)(2,1)S(1)}, u32[]{:S(2)}, u32[]{:S(2)}) %collective-permute-start) | collective-permute-done | bytes 1048608 | tf_op jit(solution)/shard_map/ppermute | solution.py:457
  110.1 2.6 %fusion.2 = bf16[64,8,2048]{2,1,0:T(8,128)(2,1)} fusion(bf16[64,8,2048]{2,1,0:T(8,128)(2,1)} %get-tuple-element.43, bf16[512,1024]{1,0:T(8,128)(2,1)S(1)} %collective-permute-done), kind=kLoop, calls=%fused_computation.7 | loop fusion | flops 2097152 | bytes 3145728 | tf_op jit(solution)/shard_map/scatter | solution.py:491
  112.7 10.0 %all-to-all-start.3 = ((bf16[64,8,2048]{2,1,0:T(8,128)(2,1)}), bf16[64,8,2048]{2,1,0:T(8,128)(2,1)S(1)}, u32[]{:S(2)}, u32[]{:S(2)}) async-start(bf16[64,8,2048]{2,1,0:T(8,128)(2,1)} %fusion.2), calls=%async_computation.3 | async-start | bytes 4194304 | tf_op jit(solution)/shard_map/all_to_all | solution.py:453
  122.8 0.7 collective-permute-start.1
  123.5 0.8 collective-permute-done.1
  124.3 26.4 %all-to-all-done.3 = bf16[64,8,2048]{2,1,0:T(8,128)(2,1)S(1)} async-done(((bf16[64,8,2048]{2,1,0:T(8,128)(2,1)}), bf16[64,8,2048]{2,1,0:T(8,128)(2,1)S(1)}, u32[]{:S(2)}, u32[]{:S(2)}) %all-to-all-start.3) | async-done | bytes 2097184 | tf_op jit(solution)/shard_map/all_to_all | solution.py:453
  150.8 0.2 convert_reduce_fusion
  150.9 1.1 broadcast_in_dim.5
  152.0 7.9 %all-to-all-start.4 = ((bf16[64,8,1152]{2,1,0:T(8,128)(2,1)}), bf16[64,8,1152]{2,1,0:T(8,128)(2,1)S(1)}, u32[]{:S(2)}, u32[]{:S(2)}) async-start(bf16[64,8,1152]{2,1,0:T(8,128)(2,1)} %broadcast_in_dim.5), calls=%async_computation.4 | async-start | bytes 2359296 | tf_op jit(solution)/shard_map/all_to_all | solution.py:453
  159.9 0.1 fusion.4
  160.0 2.8 %pad_maximum_fusion = bf16[64,32,512]{2,1,0:T(8,128)(2,1)} fusion(bf16[64,8,512]{2,1,0:T(8,128)(2,1)S(1)} %get-tuple-element.56, bf16[64,8,512]{2,1,0:T(8,128)(2,1)S(1)} %get-tuple-element.55, bf16[64,16,512]{2,1,0:T(8,128)(2,1)} %all-to-all-done.2), kind=kLoop, calls=%fused_computation.2 | loop fusion | flops 6291456 | bytes 4194304 | tf_op jit(solution)/shard_map/concatenate | solution.py:495
  162.8 13.6 %all-to-all-done.4 = bf16[64,8,1152]{2,1,0:T(8,128)(2,1)S(1)} async-done(((bf16[64,8,1152]{2,1,0:T(8,128)(2,1)}), bf16[64,8,1152]{2,1,0:T(8,128)(2,1)S(1)}, u32[]{:S(2)}, u32[]{:S(2)}) %all-to-all-start.4) | async-done | bytes 1179680 | tf_op jit(solution)/shard_map/all_to_all | solution.py:453
  176.4 3.5 %collective-permute-start.2 = (bf16[512,1152]{1,0:T(8,128)(2,1)S(1)}, bf16[512,1152]{1,0:T(8,128)(2,1)S(1)}, u32[]{:S(2)}, u32[]{:S(2)}) collective-permute-start(bf16[512,1152]{1,0:T(8,128)(2,1)S(1)} %bitcast.20), channel_id=1, source_target_pairs={{0,1},{1,0},{2,3},{3,2},{4,5},{5,4},{6,7},{7,6},{8,9},{9,8},{10,11... | collective-permute-start | bytes 3538952 | tf_op jit(solution)/shard_map/ppermute | solution.py:457
  179.9 1.4 place_own.1
  181.3 0.1 convert_reduce_fusion.1
  181.4 0.6 slice_bitcast_fusion
  182.0 0.4 collective-permute-done.2.refs_1_
  182.4 1.4 place_other.1
  (16 shorter events, 0.1 us)
Async XLA Ops:
  0.6 17.1 %copy-start = (f32[16,225]{1,0:T(8,128)S(1)}, f32[16,225]{1,0:T(8,128)}, u32[]{:S(2)}) copy-start(f32[16,225]{1,0:T(8,128)} %param.15) | copy-start | bytes 43204
  3.1 39.2 %all-to-all-start = ((bf16[64,32,512]{2,1,0:T(8,128)(2,1)}), bf16[64,32,512]{2,1,0:T(8,128)(2,1)S(1)}, u32[]{:S(2)}, u32[]{:S(2)}) async-start(bf16[64,32,512]{2,1,0:T(8,128)(2,1)} %pack_part.3), calls=%async_computation | async-start | bytes 4194304 | tf_op jit(solution)/shard_map/all_to_all | solution.py:453
  20.0 30.4 %copy-start.2 = (bf16[512,512]{1,0:T(8,128)(2,1)S(1)}, bf16[512,512]{1,0:T(8,128)(2,1)}, u32[]{:S(2)}) copy-start(bf16[512,512]{1,0:T(8,128)(2,1)} %refs_1_.1) | copy-start | bytes 1572868
  42.3 33.4 %all-to-all-start.1 = ((bf16[64,32,512]{2,1,0:T(8,128)(2,1)}), bf16[64,32,512]{2,1,0:T(8,128)(2,1)}, u32[]{:S(2)}, u32[]{:S(2)}) async-start(bf16[64,32,512]{2,1,0:T(8,128)(2,1)} %pack_part.2), calls=%async_computation.1 | async-start | bytes 4194304 | tf_op jit(solution)/shard_map/all_to_all | solution.py:453
  50.3 1.8 copy-start.7
  50.3 1.8 copy-start.8
  50.4 1.4 copy-start.1
  69.4 1.1 copy-start.3
  70.5 0.7 copy-start.5
  71.2 1.9 %copy-start.9 = (f32[4,512,512]{2,1,0:T(8,128)}, f32[4,512,512]{2,1,0:T(8,128)S(1)}, u32[]{:S(2)}) copy-start(f32[4,512,512]{2,1,0:T(8,128)S(1)} %get-tuple-element.41.refs_8_) | copy-start | bytes 12582916
  75.7 9.5 %copy-start.4 = (bf16[512,1536]{1,0:T(8,128)(2,1)S(1)}, bf16[512,1536]{1,0:T(8,128)(2,1)}, u32[]{:S(2)}) copy-start(bf16[512,1536]{1,0:T(8,128)(2,1)} %copy-done.3) | copy-start | bytes 4718596
  75.7 29.0 %all-to-all-start.2 = ((bf16[64,16,512]{2,1,0:T(8,128)(2,1)}), bf16[64,16,512]{2,1,0:T(8,128)(2,1)}, u32[]{:S(2)}, u32[]{:S(2)}) async-start(bf16[64,16,512]{2,1,0:T(8,128)(2,1)} %get-tuple-element.46), calls=%async_computation.2 | async-start | bytes 2097152 | tf_op jit(solution)/shard_map/all_to_all | solution.py:453
  85.2 1.0 copy-start.6
  104.7 5.4 %collective-permute-start = (bf16[512,1024]{1,0:T(8,128)(2,1)S(1)}, bf16[512,1024]{1,0:T(8,128)(2,1)S(1)}, u32[]{:S(2)}, u32[]{:S(2)}) collective-permute-start(bf16[512,1024]{1,0:T(8,128)(2,1)S(1)} %get-tuple-element.47), channel_id=1, source_target_pairs={{0,1},{1,0},{2,3},{3,2},{4,5},{5,4},{6,7},{7,6},{8,9},{9,8},{10,11... | collective-permute-start | bytes 3145736 | tf_op jit(solution)/shard_map/ppermute | solution.py:457
  112.7 38.1 %all-to-all-start.3 = ((bf16[64,8,2048]{2,1,0:T(8,128)(2,1)}), bf16[64,8,2048]{2,1,0:T(8,128)(2,1)S(1)}, u32[]{:S(2)}, u32[]{:S(2)}) async-start(bf16[64,8,2048]{2,1,0:T(8,128)(2,1)} %fusion.2), calls=%async_computation.3 | async-start | bytes 4194304 | tf_op jit(solution)/shard_map/all_to_all | solution.py:453
  122.8 1.6 collective-permute-start.1
  152.0 24.4 %all-to-all-start.4 = ((bf16[64,8,1152]{2,1,0:T(8,128)(2,1)}), bf16[64,8,1152]{2,1,0:T(8,128)(2,1)S(1)}, u32[]{:S(2)}, u32[]{:S(2)}) async-start(bf16[64,8,1152]{2,1,0:T(8,128)(2,1)} %broadcast_in_dim.5), calls=%async_computation.4 | async-start | bytes 2359296 | tf_op jit(solution)/shard_map/all_to_all | solution.py:453
  176.4 5.9 %collective-permute-start.2 = (bf16[512,1152]{1,0:T(8,128)(2,1)S(1)}, bf16[512,1152]{1,0:T(8,128)(2,1)S(1)}, u32[]{:S(2)}, u32[]{:S(2)}) collective-permute-start(bf16[512,1152]{1,0:T(8,128)(2,1)S(1)} %bitcast.20), channel_id=1, source_target_pairs={{0,1},{1,0},{2,3},{3,2},{4,5},{5,4},{6,7},{7,6},{8,9},{9,8},{10,11... | collective-permute-start | bytes 3538952 | tf_op jit(solution)/shard_map/ppermute | solution.py:457

commit v6 on v5

--- a/solution.py
+++ b/solution.py
@@ -266,8 +266,8 @@
             pltpu.VMEM(x.shape, BF16),
             pltpu.VMEM(grads.shape, F32),
             pltpu.VMEM(outs[0].shape, BF16),
-            pltpu.VMEM((4, cells, 128), F32),
-            pltpu.VMEM((4, cells, 128), F32),
+            pltpu.VMEM((4, cells + windows, 128), F32),
+            pltpu.VMEM((4, cells + windows, 128), F32),
             pltpu.VMEM((ROWS, 1536), BF16),
             pltpu.VMEM((ROWS, 512), BF16),
             pltpu.VMEM((ROWS, 1536), BF16),

time: 185 us -> 185 us (level)
  no operation moved by 1% of the time
where the time goes in v6:
time: 185 us; the launch traced here: 184 us
  waiting for transfers between devices  68.5 us (37%)
  starting transfers between devices  54.7 us (30%)
  Pallas kernels  43.7 us (24%)
  local copies, waits for them, and re-layouts  8.91 us (5%)
  other arithmetic  5.76 us (3%)
    all_to_all x5, waiting for transfers between devices, exchange(): lax.all_to_all(array, ('gx', 'gh'), split_axis=0, concat_axis=0, tiled=True)  65 us
    all_to_all x5, starting transfers between devices, exchange(): lax.all_to_all(array, ('gx', 'gh'), split_axis=0, concat_axis=0, tiled=True)  47.4 us
    pallas_call x2, Pallas kernels, window_pass(): pl.pallas_call(kernel, in_specs=[pl.BlockSpec(memory_space=pltpu.SMEM), h...  35.7 us
    ppermute x3, starting transfers between devices, swap_cores(): return lax.ppermute(array, 'core', [(0, 1), (1, 0)])  7.28 us
    unnamed x20, local copies, waits for them, and re-layouts  6.15 us
    pallas_call x2, Pallas kernels, pack(): pl.pallas_call(kernel, in_specs=[hbm, hbm], out_specs=hbm, out_shape=jax....  4.9 us
  transfers between devices with their start and end apart: 8, of which 7 were waited for; matrix products, arithmetic and copies ran while one was open for 3% of the time, Pallas kernels for 22%

profile of v6, /device:TPU:1, one launch (start us, length us, event | category | flops | bytes accessed | tf_op | source)
XLA Modules:
  0.0 184.0 jit_solution(13192686360326772516)
XLA Ops:
  0.6 0.0 copy-start
  0.6 2.4 %pack_part.3 = bf16[64,32,512]{2,1,0:T(8,128)(2,1)} custom-call(bf16[64,32,512]{2,1,0:T(8,128)(2,1)} %bitcast.26, bf16[64,32,512]{2,1,0:T(8,128)(2,1)} %bitcast.28), custom_call_target="tpu_custom_call" | custom-call | bytes 4194304 | tf_op jit(solution)/shard_map/pack_part/pallas_call | solution.py:350
  3.1 12.0 %all-to-all-start = ((bf16[64,32,512]{2,1,0:T(8,128)(2,1)}), bf16[64,32,512]{2,1,0:T(8,128)(2,1)S(1)}, u32[]{:S(2)}, u32[]{:S(2)}) async-start(bf16[64,32,512]{2,1,0:T(8,128)(2,1)} %pack_part.3), calls=%async_computation | async-start | bytes 4194304 | tf_op jit(solution)/shard_map/all_to_all | solution.py:453
  15.1 2.4 %pack_part.2 = bf16[64,32,512]{2,1,0:T(8,128)(2,1)} custom-call(bf16[64,32,512]{2,1,0:T(8,128)(2,1)} %bitcast.27, bf16[64,32,512]{2,1,0:T(8,128)(2,1)} %bitcast.29), custom_call_target="tpu_custom_call" | custom-call | bytes 4194304 | tf_op jit(solution)/shard_map/pack_part/pallas_call | solution.py:350
  17.6 0.1 add_add_fusion
  17.6 0.1 add.66
  17.7 0.0 copy-done
  17.7 1.3 convolution_bitcast_fusion
  19.1 0.2 reshape.216
  19.3 0.3 copy.16
  19.6 0.3 reshape.217.refs_2_
  20.0 0.0 copy-start.2
  20.0 22.3 %all-to-all-done.refs_1_ = bf16[64,32,512]{2,1,0:T(8,128)(2,1)S(1)} async-done(((bf16[64,32,512]{2,1,0:T(8,128)(2,1)}), bf16[64,32,512]{2,1,0:T(8,128)(2,1)S(1)}, u32[]{:S(2)}, u32[]{:S(2)}) %all-to-all-start) | async-done | bytes 2097184 | tf_op jit(solution)/shard_map/all_to_all | solution.py:453
  42.3 8.0 %all-to-all-start.1 = ((bf16[64,32,512]{2,1,0:T(8,128)(2,1)}), bf16[64,32,512]{2,1,0:T(8,128)(2,1)}, u32[]{:S(2)}, u32[]{:S(2)}) async-start(bf16[64,32,512]{2,1,0:T(8,128)(2,1)} %pack_part.2), calls=%async_computation.1 | async-start | bytes 4194304 | tf_op jit(solution)/shard_map/all_to_all | solution.py:453
  50.3 0.0 copy-start.7
  50.3 0.0 copy-start.8
  50.4 0.0 copy-start.1
  50.4 1.4 copy-done.1
  51.8 0.3 stage_constants.1
  52.1 17.2 %window_first.1 = (bf16[64,16,512]{2,1,0:T(8,128)(2,1)}, f32[4,512,512]{2,1,0:T(8,128)S(1)}, f32[2,8,512]{2,1,0:T(8,128)S(1)}) custom-call(s32[1]{0:T(128)} %bitcast.refs_0_, bf16[64,32,512]{2,1,0:T(8,128)(2,1)S(1)} %all-to-all-done.refs_1_, f32[1,512]{1,0:T(1,128)S(1)} %bitcast.22, f32[1,512]{1,0:T(1,128)S(1)} %bitcast.24, ...), custom_call_target="tpu_custom_call" | custom-call | flops 20000000000 | bytes 12582912 | tf_op jit(solution)/shard_map/window_first/pallas_call | solution.py:256
  69.4 0.0 copy-start.3
  69.4 1.1 copy-done.3
  70.5 0.7 copy-done.5
  71.2 1.9 %copy-done.9 = f32[4,512,512]{2,1,0:T(8,128)} copy-done((f32[4,512,512]{2,1,0:T(8,128)}, f32[4,512,512]{2,1,0:T(8,128)S(1)}, u32[]{:S(2)}) %copy-start.9) | copy-done | bytes 4194328
  73.1 2.6 %all-to-all-done.1.refs_1_ = bf16[64,32,512]{2,1,0:T(8,128)(2,1)} async-done(((bf16[64,32,512]{2,1,0:T(8,128)(2,1)}), bf16[64,32,512]{2,1,0:T(8,128)(2,1)}, u32[]{:S(2)}, u32[]{:S(2)}) %all-to-all-start.1) | async-done | bytes 2097184 | tf_op jit(solution)/shard_map/all_to_all | solution.py:453
  75.7 9.5 %all-to-all-start.2 = ((bf16[64,16,512]{2,1,0:T(8,128)(2,1)}), bf16[64,16,512]{2,1,0:T(8,128)(2,1)}, u32[]{:S(2)}, u32[]{:S(2)}) async-start(bf16[64,16,512]{2,1,0:T(8,128)(2,1)} %get-tuple-element.46), calls=%async_computation.2 | async-start | bytes 2097152 | tf_op jit(solution)/shard_map/all_to_all | solution.py:453
  85.3 0.9 copy-done.6
  86.2 18.5 %window_last.1 = (bf16[64,8,2048]{2,1,0:T(8,128)(2,1)}, bf16[512,1024]{1,0:T(8,128)(2,1)S(1)}, f32[8,128]{1,0:T(8,128)S(1)}) custom-call(s32[1]{0:T(128)} %bitcast.refs_0_, bf16[64,32,512]{2,1,0:T(8,128)(2,1)} %all-to-all-done.1.refs_1_, f32[1,512]{1,0:T(1,128)S(1)} %bitcast.23, f32[1,512]{1,0:T(1,128)S(1)} %bitcast.25, bf16[512,1536]{1,0:T(8,128)(2,1)S(1)} %copy-done.4, ...), custom_call_target="tpu_custom_call" | custom-call | flops 20000000000 | bytes 12582912 | tf_op jit(solution)/shard_map/window_last/pallas_call | solution.py:256
  104.7 0.0 all-to-all-done.2
  104.7 3.1 %collective-permute-start = (bf16[512,1024]{1,0:T(8,128)(2,1)S(1)}, bf16[512,1024]{1,0:T(8,128)(2,1)S(1)}, u32[]{:S(2)}, u32[]{:S(2)}) collective-permute-start(bf16[512,1024]{1,0:T(8,128)(2,1)S(1)} %get-tuple-element.47), channel_id=1, source_target_pairs={{0,1},{1,0},{2,3},{3,2},{4,5},{5,4},{6,7},{7,6},{8,9},{9,8},{10,11... | collective-permute-start | bytes 3145736 | tf_op jit(solution)/shard_map/ppermute | solution.py:457
  107.8 2.3 %collective-permute-done = bf16[512,1024]{1,0:T(8,128)(2,1)S(1)} collective-permute-done((bf16[512,1024]{1,0:T(8,128)(2,1)S(1)}, bf16[512,1024]{1,0:T(8,128)(2,1)S(1)}, u32[]{:S(2)}, u32[]{:S(2)}) %collective-permute-start) | collective-permute-done | bytes 1048608 | tf_op jit(solution)/shard_map/ppermute | solution.py:457
  110.1 2.6 %fusion.2 = bf16[64,8,2048]{2,1,0:T(8,128)(2,1)} fusion(bf16[64,8,2048]{2,1,0:T(8,128)(2,1)} %get-tuple-element.43, bf16[512,1024]{1,0:T(8,128)(2,1)S(1)} %collective-permute-done), kind=kLoop, calls=%fused_computation.7 | loop fusion | flops 2097152 | bytes 3145728 | tf_op jit(solution)/shard_map/scatter | solution.py:491
  112.7 10.0 %all-to-all-start.3 = ((bf16[64,8,2048]{2,1,0:T(8,128)(2,1)}), bf16[64,8,2048]{2,1,0:T(8,128)(2,1)S(1)}, u32[]{:S(2)}, u32[]{:S(2)}) async-start(bf16[64,8,2048]{2,1,0:T(8,128)(2,1)} %fusion.2), calls=%async_computation.3 | async-start | bytes 4194304 | tf_op jit(solution)/shard_map/all_to_all | solution.py:453
  122.8 0.7 collective-permute-start.1
  123.5 0.8 collective-permute-done.1
  124.3 26.4 %all-to-all-done.3 = bf16[64,8,2048]{2,1,0:T(8,128)(2,1)S(1)} async-done(((bf16[64,8,2048]{2,1,0:T(8,128)(2,1)}), bf16[64,8,2048]{2,1,0:T(8,128)(2,1)S(1)}, u32[]{:S(2)}, u32[]{:S(2)}) %all-to-all-start.3) | async-done | bytes 2097184 | tf_op jit(solution)/shard_map/all_to_all | solution.py:453
  150.8 0.2 convert_reduce_fusion
  150.9 1.1 broadcast_in_dim.5
  152.0 7.9 %all-to-all-start.4 = ((bf16[64,8,1152]{2,1,0:T(8,128)(2,1)}), bf16[64,8,1152]{2,1,0:T(8,128)(2,1)S(1)}, u32[]{:S(2)}, u32[]{:S(2)}) async-start(bf16[64,8,1152]{2,1,0:T(8,128)(2,1)} %broadcast_in_dim.5), calls=%async_computation.4 | async-start | bytes 2359296 | tf_op jit(solution)/shard_map/all_to_all | solution.py:453
  159.9 0.1 fusion.4
  160.0 2.8 %pad_maximum_fusion = bf16[64,32,512]{2,1,0:T(8,128)(2,1)} fusion(bf16[64,8,512]{2,1,0:T(8,128)(2,1)S(1)} %get-tuple-element.56, bf16[64,8,512]{2,1,0:T(8,128)(2,1)S(1)} %get-tuple-element.55, bf16[64,16,512]{2,1,0:T(8,128)(2,1)} %all-to-all-done.2), kind=kLoop, calls=%fused_computation.2 | loop fusion | flops 6291456 | bytes 4194304 | tf_op jit(solution)/shard_map/concatenate | solution.py:495
  162.8 13.6 %all-to-all-done.4 = bf16[64,8,1152]{2,1,0:T(8,128)(2,1)S(1)} async-done(((bf16[64,8,1152]{2,1,0:T(8,128)(2,1)}), bf16[64,8,1152]{2,1,0:T(8,128)(2,1)S(1)}, u32[]{:S(2)}, u32[]{:S(2)}) %all-to-all-start.4) | async-done | bytes 1179680 | tf_op jit(solution)/shard_map/all_to_all | solution.py:453
  176.4 3.5 %collective-permute-start.2 = (bf16[512,1152]{1,0:T(8,128)(2,1)S(1)}, bf16[512,1152]{1,0:T(8,128)(2,1)S(1)}, u32[]{:S(2)}, u32[]{:S(2)}) collective-permute-start(bf16[512,1152]{1,0:T(8,128)(2,1)S(1)} %bitcast.20), channel_id=1, source_target_pairs={{0,1},{1,0},{2,3},{3,2},{4,5},{5,4},{6,7},{7,6},{8,9},{9,8},{10,11... | collective-permute-start | bytes 3538952 | tf_op jit(solution)/shard_map/ppermute | solution.py:457
  179.9 1.4 place_own.1
  181.3 0.1 convert_reduce_fusion.1
  181.4 0.6 slice_bitcast_fusion
  182.0 0.4 collective-permute-done.2.refs_1_
  182.4 1.4 place_other.1
  (16 shorter events, 0.1 us)
Async XLA Ops:
  0.6 17.1 %copy-start = (f32[16,225]{1,0:T(8,128)S(1)}, f32[16,225]{1,0:T(8,128)}, u32[]{:S(2)}) copy-start(f32[16,225]{1,0:T(8,128)} %param.15) | copy-start | bytes 43204
  3.1 39.2 %all-to-all-start = ((bf16[64,32,512]{2,1,0:T(8,128)(2,1)}), bf16[64,32,512]{2,1,0:T(8,128)(2,1)S(1)}, u32[]{:S(2)}, u32[]{:S(2)}) async-start(bf16[64,32,512]{2,1,0:T(8,128)(2,1)} %pack_part.3), calls=%async_computation | async-start | bytes 4194304 | tf_op jit(solution)/shard_map/all_to_all | solution.py:453
  20.0 30.4 %copy-start.2 = (bf16[512,512]{1,0:T(8,128)(2,1)S(1)}, bf16[512,512]{1,0:T(8,128)(2,1)}, u32[]{:S(2)}) copy-start(bf16[512,512]{1,0:T(8,128)(2,1)} %refs_1_.1) | copy-start | bytes 1572868
  42.3 33.4 %all-to-all-start.1 = ((bf16[64,32,512]{2,1,0:T(8,128)(2,1)}), bf16[64,32,512]{2,1,0:T(8,128)(2,1)}, u32[]{:S(2)}, u32[]{:S(2)}) async-start(bf16[64,32,512]{2,1,0:T(8,128)(2,1)} %pack_part.2), calls=%async_computation.1 | async-start | bytes 4194304 | tf_op jit(solution)/shard_map/all_to_all | solution.py:453
  50.3 1.8 copy-start.7
  50.3 1.8 copy-start.8
  50.4 1.4 copy-start.1
  69.4 1.1 copy-start.3
  70.5 0.7 copy-start.5
  71.2 1.9 %copy-start.9 = (f32[4,512,512]{2,1,0:T(8,128)}, f32[4,512,512]{2,1,0:T(8,128)S(1)}, u32[]{:S(2)}) copy-start(f32[4,512,512]{2,1,0:T(8,128)S(1)} %get-tuple-element.41.refs_8_) | copy-start | bytes 12582916
  75.7 9.5 %copy-start.4 = (bf16[512,1536]{1,0:T(8,128)(2,1)S(1)}, bf16[512,1536]{1,0:T(8,128)(2,1)}, u32[]{:S(2)}) copy-start(bf16[512,1536]{1,0:T(8,128)(2,1)} %copy-done.3) | copy-start | bytes 4718596
  75.7 29.0 %all-to-all-start.2 = ((bf16[64,16,512]{2,1,0:T(8,128)(2,1)}), bf16[64,16,512]{2,1,0:T(8,128)(2,1)}, u32[]{:S(2)}, u32[]{:S(2)}) async-start(bf16[64,16,512]{2,1,0:T(8,128)(2,1)} %get-tuple-element.46), calls=%async_computation.2 | async-start | bytes 2097152 | tf_op jit(solution)/shard_map/all_to_all | solution.py:453
  85.2 1.0 copy-start.6
  104.7 5.4 %collective-permute-start = (bf16[512,1024]{1,0:T(8,128)(2,1)S(1)}, bf16[512,1024]{1,0:T(8,128)(2,1)S(1)}, u32[]{:S(2)}, u32[]{:S(2)}) collective-permute-start(bf16[512,1024]{1,0:T(8,128)(2,1)S(1)} %get-tuple-element.47), channel_id=1, source_target_pairs={{0,1},{1,0},{2,3},{3,2},{4,5},{5,4},{6,7},{7,6},{8,9},{9,8},{10,11... | collective-permute-start | bytes 3145736 | tf_op jit(solution)/shard_map/ppermute | solution.py:457
  112.7 38.1 %all-to-all-start.3 = ((bf16[64,8,2048]{2,1,0:T(8,128)(2,1)}), bf16[64,8,2048]{2,1,0:T(8,128)(2,1)S(1)}, u32[]{:S(2)}, u32[]{:S(2)}) async-start(bf16[64,8,2048]{2,1,0:T(8,128)(2,1)} %fusion.2), calls=%async_computation.3 | async-start | bytes 4194304 | tf_op jit(solution)/shard_map/all_to_all | solution.py:453
  122.8 1.6 collective-permute-start.1
  152.0 24.4 %all-to-all-start.4 = ((bf16[64,8,1152]{2,1,0:T(8,128)(2,1)}), bf16[64,8,1152]{2,1,0:T(8,128)(2,1)S(1)}, u32[]{:S(2)}, u32[]{:S(2)}) async-start(bf16[64,8,1152]{2,1,0:T(8,128)(2,1)} %broadcast_in_dim.5), calls=%async_computation.4 | async-start | bytes 2359296 | tf_op jit(solution)/shard_map/all_to_all | solution.py:453
  176.4 5.9 %collective-permute-start.2 = (bf16[512,1152]{1,0:T(8,128)(2,1)S(1)}, bf16[512,1152]{1,0:T(8,128)(2,1)S(1)}, u32[]{:S(2)}, u32[]{:S(2)}) collective-permute-start(bf16[512,1152]{1,0:T(8,128)(2,1)S(1)} %bitcast.20), channel_id=1, source_target_pairs={{0,1},{1,0},{2,3},{3,2},{4,5},{5,4},{6,7},{7,6},{8,9},{9,8},{10,11... | collective-permute-start | bytes 3538952 | tf_op jit(solution)/shard_map/ppermute | solution.py:457
